TPU v7x, 32 devices: a whole 2x2x4 slice. The times are simulated.
32 devices in a mesh: tile: 8 (over y, x, core), vis: 4 (over z).
Axes of the slice: x: 2, y: 2, z: 4, core: 2. Of those that a mesh axis runs over, the one named last changes fastest.
Arguments:
- pieces: float32 [1024, 16, 1024], P(('tile', 'vis')), may hold values from -6 to 6
- coeffs: float32 [1024, 5, 4], P(('tile', 'vis')), may hold values from -1.8 to 1.8
- weights: float32 [1024], P(('tile', 'vis')), may hold values from 0.1 to 1
- routes: int32 [1024, 1], P(('tile', 'vis')), may hold values from 0 to 7; in each aligned block of 32 rows (0 to 31, 32 to 63, ...) at most 8 rows name the same one
- offsets: int32 [1024], P(('tile', 'vis')), may hold values from 0 to 63
Outputs:
- coadd: float32 [8192, 1024], P(('tile', 'vis'))
- detection: float32 [8192, 1024], P(('tile', 'vis'))
Inputs may be any that keep to these rules, and one draw needn't show every extreme that they name: `routes`: among the 32 pieces of one device no strip index appears more than 8 times, and some index appears exactly 8 times; every strip index appears somewhere.
All inputs are finite; a program needn't handle non-finite values.
Results may differ from a plain program's by a relative error of at most 0.0003.
Values sent between devices are 32-bit elements; how exact they have to be, the bound alone decides.
A program may use at most 128 MiB of HBM per device.

v0:
```python
import jax
import jax.numpy as jnp
from jax import lax
from jax.sharding import PartitionSpec as P

SR = 1024
TAPS = 10
REACH = 15


row_shapes = ((1.0, 0), (1.0, 1), (2.0, 0), (2.0, 2), (3.5, 0))
column_shapes = ((1.0, 0), (2.0, 0), (2.0, 1), (3.5, 0))
highest = lax.Precision.HIGHEST


def extended(cells, sides, width):
    for axis, dim in sides:
        count = lax.axis_size(axis)
        ends = count - 1
        head = lax.slice_in_dim(cells, 0, width, axis=dim)
        tail = lax.slice_in_dim(cells, cells.shape[dim] - width, cells.shape[dim], axis=dim)
        cells = jnp.concatenate(
            [
                lax.ppermute(tail, axis, [(i, (i + 1) % count) for i in range(ends)]),
                cells,
                lax.ppermute(head, axis, [((i + 1) % count, i) for i in range(ends)]),
            ],
            axis=dim,
        )
    return cells


def shaped_taps(lag_table, shape_list, tap_reach):
    tap_spots = jnp.arange(-tap_reach, tap_reach + 1).astype(jnp.float32)
    lagged = lag_table.astype(jnp.float32)
    stacked = []
    for spread, degree in shape_list:
        full_taps = (
            jnp.exp(-tap_spots * tap_spots / (2.0 * spread * spread))
            * (tap_spots / spread) ** degree
        )
        unit_scale = 1.0 / jnp.sqrt(jnp.sum(full_taps * full_taps))
        values = (
            jnp.exp(-lagged * lagged / (2.0 * spread * spread))
            * (lagged / spread) ** degree
            * unit_scale
        )
        stacked.append(jnp.where(jnp.abs(lag_table) <= tap_reach, values, 0.0))
    return jnp.stack(stacked)


def detect_taps(lag_table, tap_reach):
    tap_spots = jnp.arange(-tap_reach, tap_reach + 1).astype(jnp.float32)
    gauss_total = jnp.sum(jnp.exp(-tap_spots * tap_spots / 18.0))
    lagged = lag_table.astype(jnp.float32)
    values = jnp.exp(-lagged * lagged / 18.0) / gauss_total - 1.0 / (2 * tap_reach + 1)
    return jnp.where(jnp.abs(lag_table) <= tap_reach, values, 0.0)


def basis_tables(piece_rows):
    row_lag = jnp.arange(piece_rows)[None, :] - jnp.arange(piece_rows)[:, None]
    row_bank = shaped_taps(row_lag, row_shapes, TAPS)
    column_lag = jnp.arange(384)[:, None] - 128 - jnp.arange(128)[None, :]
    column_windows = shaped_taps(column_lag, column_shapes, TAPS)
    detect_windows = detect_taps(column_lag, REACH)[None]
    return (row_bank, column_windows, detect_windows)


def column_pass(images, windows):
    lead_count, kernel_count, rows_count, strip_width = images.shape
    blocks = strip_width // 128
    padded = jnp.pad(images, ((0, 0), (0, 0), (0, 0), (128, 128)))
    viewed = padded.reshape(lead_count, kernel_count, rows_count, blocks + 2, 128)
    framed = jnp.concatenate(
        [
            viewed[:, :, :, 0:blocks],
            viewed[:, :, :, 1 : blocks + 1],
            viewed[:, :, :, 2 : blocks + 2],
        ],
        axis=4,
    )
    result = jnp.einsum("mnrjk,nko->mrjo", framed, windows, precision=highest)
    return result.reshape(lead_count, rows_count, strip_width)


def match_pieces(images, factors, row_bank, column_windows):
    rowed = jnp.einsum("aqp,mpc->maqc", row_bank, images, precision=highest)
    mixed = jnp.einsum("mab,maqc->mbqc", factors, rowed, precision=highest)
    return column_pass(mixed, column_windows)


def match_grouped(images, factors, row_bank, column_windows):
    piece_count, piece_rows, strip_width = images.shape
    groups = piece_count // 8
    grouped = (
        images.reshape(groups, 8, piece_rows, strip_width),
        factors.reshape(groups, 8, factors.shape[1], factors.shape[2]),
    )

    def one_group(group_pair):
        return match_pieces(group_pair[0], group_pair[1], row_bank, column_windows)

    matched = lax.map(one_group, grouped)
    return matched.reshape(piece_count, piece_rows, strip_width)


def normalized(summed_image, weight_sums, piece_rows):
    rows_count, strip_width = summed_image.shape
    shaped = summed_image.reshape(rows_count // piece_rows, piece_rows, strip_width)
    has_weight = weight_sums > 0.0
    divisor = jnp.where(has_weight, weight_sums, 1.0)
    result = jnp.where(has_weight[:, None, None], shaped / divisor[:, None, None], 0.0)
    return result.reshape(rows_count, strip_width)


def shards(pieces, coeffs, weights, routes, offsets):
    tile_count = lax.axis_size("tile")
    group_count = lax.axis_size("vis")
    piece_count, piece_rows, strip_width = pieces.shape
    capacity = max(2, 2 * piece_count // tile_count)
    strip_rows = SR
    blocks_strip = strip_rows // piece_rows
    row_bank, column_windows, detect_windows = basis_tables(piece_rows)
    target = routes[:, 0]
    earlier = jnp.arange(piece_count)[None, :] < jnp.arange(piece_count)[:, None]
    same_target = target[:, None] == target[None, :]
    place_rank = jnp.sum(jnp.where(same_target & earlier, 1, 0), axis=1)
    slot_of = target * capacity + place_rank
    slot_hits = slot_of[None, :] == jnp.arange(tile_count * capacity)[:, None]
    filled = jnp.any(slot_hits, axis=1)
    source = jnp.sum(jnp.where(slot_hits, jnp.arange(piece_count)[None, :], 0), axis=1)
    block_hit = jnp.where(
        offsets[:, None] == jnp.arange(blocks_strip)[None, :], weights[:, None], 0.0
    )
    slot_weights = jnp.where(filled[:, None], jnp.take(block_hit, source, axis=0), 0.0)
    slot_weights = slot_weights.reshape(tile_count, capacity, blocks_strip)
    matched = match_grouped(pieces, coeffs, row_bank, column_windows)
    sent_images = jnp.where(filled[:, None, None], jnp.take(matched, source, axis=0), 0.0)
    sent_images = sent_images.reshape(tile_count, capacity, piece_rows, strip_width)
    arrived, masses = (
        lax.all_to_all(sent_images, "tile", split_axis=0, concat_axis=0, tiled=True),
        lax.all_to_all(slot_weights, "tile", split_axis=0, concat_axis=0, tiled=True),
    )
    landed = arrived.reshape(-1, piece_rows, strip_width)
    slot_mass = masses.reshape(-1, blocks_strip)
    numerator = jnp.einsum("sb,src->brc", slot_mass, landed, precision=highest).reshape(
        strip_rows, strip_width
    )
    weight_total = jnp.sum(slot_mass, axis=0)
    quarter = strip_rows // group_count
    summed_image, weight_sums = lax.psum((numerator, weight_total), "vis")
    coadd_strip = normalized(summed_image, weight_sums, piece_rows)
    filtered = column_pass(coadd_strip[None, None], detect_windows)[0]
    rimmed = extended(filtered, (("tile", 0),), REACH)
    first_row = lax.axis_index("vis") * quarter
    window_rows = lax.dynamic_slice_in_dim(rimmed, first_row, quarter + 2 * REACH, 0)
    coadd_part = lax.dynamic_slice_in_dim(coadd_strip, first_row, quarter, 0)
    lag_rows = jnp.arange(quarter + 2 * REACH)[None, :] - REACH - jnp.arange(quarter)[:, None]
    row_band = detect_taps(lag_rows, REACH)
    detection = jnp.dot(row_band, window_rows, precision=highest)
    return (coadd_part, detection)


def solution(mesh):
    placed = (
        P(("tile", "vis"), None, None),
        P(("tile", "vis"), None, None),
        P(("tile", "vis")),
        P(("tile", "vis"), None),
        P(("tile", "vis")),
    )
    return jax.shard_map(
        shards,
        mesh=mesh,
        in_specs=placed,
        out_specs=(P(("tile", "vis"), None), P(("tile", "vis"), None)),
        check_vma=False,
    )
```

profile of v0, /device:TPU:4, one launch (start us, length us, event | category | flops | bytes accessed | tf_op | source)
XLA Modules:
  0.0 431.3 jit_solution(8840981855551255169)
XLA Ops:
  7.2 0.9 select_reduce_fusion.1
  8.1 0.7 multiply_add_fusion
  9.1 0.7 fusion.63
  9.9 0.6 gather_fusion
  10.6 0.7 reshape.484
  11.2 4.2 all-to-all-start
  15.5 0.7 multiply_reduce_fusion.5
  16.2 0.6 multiply_reduce_fusion.4
  16.8 0.6 multiply_reduce_fusion.3
  17.4 0.7 multiply_reduce_fusion.2
  18.1 0.6 multiply_reduce_fusion.1
  18.8 0.6 multiply_reduce_fusion
  19.4 0.8 copy.47
  24.6 93.0 %while.12 = (s32[]{:T(128)}, f32[4,8,16,1024]{3,2,1,0:T(8,128)}, f32[4,8,5,4]{2,3,1,0:T(4,128)S(1)}, f32[4,8,16,1024]{3,2,1,0:T(8,128)}, f32[5,16,16]{2,1,0:T(8,...) while((s32[]{:T(128)}, f32[4,8,16,1024]{3,2,1,0:T(8,128)}, f32[4,8,5,4]{2,3,1,0:T(4,128)S(1)}, ...), condition=%wide.region_12.13_spmd, body=%wide.region_11.12_spmd.sunk | while | flops 2576351232 | bytes 40129644 | solution.py:103
  24.6 3.8 convolution_bitcast_fusion.3
  28.4 5.2 %fusion.98 = f32[8,4,16,1024]{3,1,2,0:T(4,128)S(1)} fusion(f32[8,5,16,1024]{3,2,1,0:T(8,128)S(1)} %convolution_bitcast_fusion.3, f32[4,8,5,4]{2,3,1,0:T(4,128)S(1)} %get-tuple-element.165, s32[]{:T(128)S(6)} %copy.87), kind=kOutput, calls=%fused_computation.8.clone.1 | convolution fusion | flops 31457280 | bytes 4734980 | tf_op jit(solution)/shard_map/while/body/eval_jaxpr/mab,maqc->mbqc/dot_general | solution.py:88
  34.2 2.7 reshape.487
  36.8 5.0 %fusion.99 = (f32[8,4,16,8,128]{4,3,1,2,0:T(8,128)S(1)}, f32[8,4,16,8,128]{4,3,1,2,0:T(8,128)S(1)}, f32[8,4,16,8,128]{4,3,1,2,0:T(8,128)S(1)}) fusion(f32[8,4,16,10,128]{4,3,1,2,0:T(8,128)} %reshape.487), kind=kLoop, calls=%fused_computation.133.clone.1 | loop fusion | bytes 12582912 | tf_op jit(solution)/shard_map/while/body/eval_jaxpr/slice | solution.py:76
  41.9 5.1 %fusion.100 = f32[8,16,8,128]{3,2,1,0:T(8,128)S(1)} fusion(f32[8,4,16,8,128]{4,3,1,2,0:T(8,128)S(1)} %get-tuple-element.144, f32[8,4,16,8,128]{4,3,1,2,0:T(8,128)S(1)} %get-tuple-element.145, f32[8,4,16,8,128]{4,3,1,2,0:T(8,128)S(1)} %get-tuple-element.146, f32[4,384,128]{2,1,0:T(8,128)S(1)} %get-tuple-element.168), kind=kOutput, calls=%fused_computation.11.clone.1 | convolution fusion | flops 2419064832 | bytes 7602176 | tf_op jit(solution)/shard_map/while/body/eval_jaxpr/mnrjk,nko->mrjo/dot_general | solution.py:82
  47.0 0.8 constant_dynamic-update-slice_fusion.7
  47.8 3.8 convolution_bitcast_fusion.3
  51.7 5.2 %fusion.98 = f32[8,4,16,1024]{3,1,2,0:T(4,128)S(1)} fusion(f32[8,5,16,1024]{3,2,1,0:T(8,128)S(1)} %convolution_bitcast_fusion.3, f32[4,8,5,4]{2,3,1,0:T(4,128)S(1)} %get-tuple-element.165, s32[]{:T(128)S(6)} %copy.87), kind=kOutput, calls=%fused_computation.8.clone.1 | convolution fusion | flops 31457280 | bytes 4734980 | tf_op jit(solution)/shard_map/while/body/eval_jaxpr/mab,maqc->mbqc/dot_general | solution.py:88
  57.4 2.7 reshape.487
  60.1 5.0 %fusion.99 = (f32[8,4,16,8,128]{4,3,1,2,0:T(8,128)S(1)}, f32[8,4,16,8,128]{4,3,1,2,0:T(8,128)S(1)}, f32[8,4,16,8,128]{4,3,1,2,0:T(8,128)S(1)}) fusion(f32[8,4,16,10,128]{4,3,1,2,0:T(8,128)} %reshape.487), kind=kLoop, calls=%fused_computation.133.clone.1 | loop fusion | bytes 12582912 | tf_op jit(solution)/shard_map/while/body/eval_jaxpr/slice | solution.py:76
  65.1 5.1 %fusion.100 = f32[8,16,8,128]{3,2,1,0:T(8,128)S(1)} fusion(f32[8,4,16,8,128]{4,3,1,2,0:T(8,128)S(1)} %get-tuple-element.144, f32[8,4,16,8,128]{4,3,1,2,0:T(8,128)S(1)} %get-tuple-element.145, f32[8,4,16,8,128]{4,3,1,2,0:T(8,128)S(1)} %get-tuple-element.146, f32[4,384,128]{2,1,0:T(8,128)S(1)} %get-tuple-element.168), kind=kOutput, calls=%fused_computation.11.clone.1 | convolution fusion | flops 2419064832 | bytes 7602176 | tf_op jit(solution)/shard_map/while/body/eval_jaxpr/mnrjk,nko->mrjo/dot_general | solution.py:82
  70.2 0.9 constant_dynamic-update-slice_fusion.7
  71.1 3.8 convolution_bitcast_fusion.3
  74.9 5.2 %fusion.98 = f32[8,4,16,1024]{3,1,2,0:T(4,128)S(1)} fusion(f32[8,5,16,1024]{3,2,1,0:T(8,128)S(1)} %convolution_bitcast_fusion.3, f32[4,8,5,4]{2,3,1,0:T(4,128)S(1)} %get-tuple-element.165, s32[]{:T(128)S(6)} %copy.87), kind=kOutput, calls=%fused_computation.8.clone.1 | convolution fusion | flops 31457280 | bytes 4734980 | tf_op jit(solution)/shard_map/while/body/eval_jaxpr/mab,maqc->mbqc/dot_general | solution.py:88
  80.6 2.7 reshape.487
  83.3 5.0 %fusion.99 = (f32[8,4,16,8,128]{4,3,1,2,0:T(8,128)S(1)}, f32[8,4,16,8,128]{4,3,1,2,0:T(8,128)S(1)}, f32[8,4,16,8,128]{4,3,1,2,0:T(8,128)S(1)}) fusion(f32[8,4,16,10,128]{4,3,1,2,0:T(8,128)} %reshape.487), kind=kLoop, calls=%fused_computation.133.clone.1 | loop fusion | bytes 12582912 | tf_op jit(solution)/shard_map/while/body/eval_jaxpr/slice | solution.py:76
  88.3 5.1 %fusion.100 = f32[8,16,8,128]{3,2,1,0:T(8,128)S(1)} fusion(f32[8,4,16,8,128]{4,3,1,2,0:T(8,128)S(1)} %get-tuple-element.144, f32[8,4,16,8,128]{4,3,1,2,0:T(8,128)S(1)} %get-tuple-element.145, f32[8,4,16,8,128]{4,3,1,2,0:T(8,128)S(1)} %get-tuple-element.146, f32[4,384,128]{2,1,0:T(8,128)S(1)} %get-tuple-element.168), kind=kOutput, calls=%fused_computation.11.clone.1 | convolution fusion | flops 2419064832 | bytes 7602176 | tf_op jit(solution)/shard_map/while/body/eval_jaxpr/mnrjk,nko->mrjo/dot_general | solution.py:82
  93.5 0.8 constant_dynamic-update-slice_fusion.7
  94.3 3.8 convolution_bitcast_fusion.3
  98.2 5.2 %fusion.98 = f32[8,4,16,1024]{3,1,2,0:T(4,128)S(1)} fusion(f32[8,5,16,1024]{3,2,1,0:T(8,128)S(1)} %convolution_bitcast_fusion.3, f32[4,8,5,4]{2,3,1,0:T(4,128)S(1)} %get-tuple-element.165, s32[]{:T(128)S(6)} %copy.87), kind=kOutput, calls=%fused_computation.8.clone.1 | convolution fusion | flops 31457280 | bytes 4734980 | tf_op jit(solution)/shard_map/while/body/eval_jaxpr/mab,maqc->mbqc/dot_general | solution.py:88
  103.9 2.7 reshape.487
  106.6 5.0 %fusion.99 = (f32[8,4,16,8,128]{4,3,1,2,0:T(8,128)S(1)}, f32[8,4,16,8,128]{4,3,1,2,0:T(8,128)S(1)}, f32[8,4,16,8,128]{4,3,1,2,0:T(8,128)S(1)}) fusion(f32[8,4,16,10,128]{4,3,1,2,0:T(8,128)} %reshape.487), kind=kLoop, calls=%fused_computation.133.clone.1 | loop fusion | bytes 12582912 | tf_op jit(solution)/shard_map/while/body/eval_jaxpr/slice | solution.py:76
  111.6 5.1 %fusion.100 = f32[8,16,8,128]{3,2,1,0:T(8,128)S(1)} fusion(f32[8,4,16,8,128]{4,3,1,2,0:T(8,128)S(1)} %get-tuple-element.144, f32[8,4,16,8,128]{4,3,1,2,0:T(8,128)S(1)} %get-tuple-element.145, f32[8,4,16,8,128]{4,3,1,2,0:T(8,128)S(1)} %get-tuple-element.146, f32[4,384,128]{2,1,0:T(8,128)S(1)} %get-tuple-element.168), kind=kOutput, calls=%fused_computation.11.clone.1 | convolution fusion | flops 2419064832 | bytes 7602176 | tf_op jit(solution)/shard_map/while/body/eval_jaxpr/mnrjk,nko->mrjo/dot_general | solution.py:82
  116.7 0.9 constant_dynamic-update-slice_fusion.7
  117.6 4.3 %gather_fusion.1 = f32[64,16,1024]{2,1,0:T(8,128)} fusion(f32[32,16,1024]{2,1,0:T(8,128)} %bitcast.87, s32[1024]{0:T(1024)S(1)} %pad_clamp_fusion), kind=kCustom, calls=%fused_computation.1 | custom fusion | bytes 8388864 | tf_op jit(solution)/shard_map/jit(_take)/gather | solution.py:138
  121.9 7.5 %fusion.25 = f32[8,8,16,1024]{3,1,2,0:T(8,128)} fusion(f32[8,8,16,1024]{3,2,1,0:T(8,128)} %bitcast.84, pred[8,8]{1,0:T(8,128)(4,1)S(1)} %compare_and_fusion, pred[8,8]{1,0:T(8,128)(4,1)S(1)} %broadcast_in_dim.147), kind=kLoop, calls=%fused_computation.29 | loop fusion | flops 2097152 | bytes 8388736 | tf_op jit(solution)/shard_map/jit(_where)/select_n | solution.py:138
  129.4 4.5 %all-to-all-start.1 = ((f32[8,8,16,1024]{3,1,2,0:T(8,128)}), f32[8,8,16,1024]{3,1,2,0:T(8,128)}, u32[]{:S(2)}, u32[]{:S(2)}) async-start(f32[8,8,16,1024]{3,1,2,0:T(8,128)} %fusion.25), calls=%async_computation.1 | async-start | bytes 8388608 | tf_op jit(solution)/shard_map/all_to_all | solution.py:141
  134.5 0.7 reduce.1
  135.3 46.4 %all-to-all-done.1 = f32[8,8,16,1024]{3,1,2,0:T(8,128)} async-done(((f32[8,8,16,1024]{3,1,2,0:T(8,128)}), f32[8,8,16,1024]{3,1,2,0:T(8,128)}, u32[]{:S(2)}, u32[]{:S(2)}) %all-to-all-start.1) | async-done | bytes 4194336 | tf_op jit(solution)/shard_map/all_to_all | solution.py:141
  181.7 5.7 %convolution_bitcast_fusion.1 = f32[64,16,1024]{2,0,1:T(8,128)S(1)} fusion(f32[8,8,16,1024]{3,1,2,0:T(8,128)} %all-to-all-done.1, f32[8,8,64]{2,1,0:T(8,128)S(1)} %reshape.485), kind=kOutput, calls=%fused_computation.31 | convolution fusion | flops 805306368 | bytes 8404992 | tf_op jit(solution)/shard_map/sb,src->brc/dot_general | solution.py:146
  187.4 4.4 %copy.50 = f32[64,16,1024]{2,1,0:T(8,128)} copy(f32[64,16,1024]{2,0,1:T(8,128)S(1)} %convolution_bitcast_fusion.1) | data formatting | bytes 8388608 | tf_op jit(solution)/shard_map/sb,src->brc/dot_general | solution.py:146
  191.8 0.6 fusion.66
  192.5 12.2 %psum.14 = f32[64]{0:T(128)S(1)} all-reduce(f32[64]{0:T(128)S(1)} %reduce_sum.114), channel_id=1, replica_groups=mesh['tile'=8,'vis'=4] {'vis'}, use_global_device_ids=true, to_apply=%region_4.5 | all-reduce | flops 64 | bytes 512 | tf_op jit(solution)/shard_map/psum | solution.py:151
  205.1 142.3 %all-reduce.4.cloned.1.call-done = f32[1024,1024]{1,0:T(8,128)} async-done(((f32[1024,1024]{1,0:T(8,128)}), f32[1024,1024]{1,0:T(8,128)}) %all-reduce.4.cloned.1.call-update) | async-done | bytes 4194320 | tf_op jit(solution)/shard_map/psum | solution.py:151
  347.4 4.0 fusion.82
  351.3 5.3 %copy.71 = f32[1,1,1024,1024]{2,3,1,0:T(8,128)} copy(f32[1,1,1024,1024]{3,2,1,0:T(8,128)} %fusion.82) | data formatting | bytes 8388608
  356.7 2.6 pad.11.clone
  359.3 4.7 %fusion.79 = (f32[1,1,1024,8,128]{2,4,3,1,0:T(8,128)}, f32[1,1,1024,8,128]{2,4,3,1,0:T(8,128)}, f32[1,1,1024,8,128]{2,4,3,1,0:T(8,128)}) fusion(f32[1,1,1024,10,128]{2,4,3,1,0:T(8,128)S(1)} %bitcast.83), kind=kLoop, calls=%fused_computation.134 | loop fusion | bytes 25165824 | tf_op jit(solution)/shard_map/slice | solution.py:76
  364.1 5.3 %copy.70 = f32[1,1,1024,8,128]{4,2,3,1,0:T(8,128)} copy(f32[1,1,1024,8,128]{2,4,3,1,0:T(8,128)} %get-tuple-element.97) | data formatting | bytes 8388608
  369.4 5.3 %copy.69 = f32[1,1,1024,8,128]{4,2,3,1,0:T(8,128)} copy(f32[1,1,1024,8,128]{2,4,3,1,0:T(8,128)} %get-tuple-element.96) | data formatting | bytes 8388608
  374.7 5.3 %copy.68 = f32[1,1,1024,8,128]{4,2,3,1,0:T(8,128)} copy(f32[1,1,1024,8,128]{2,4,3,1,0:T(8,128)} %get-tuple-element.95) | data formatting | bytes 8388608
  380.0 14.3 %fusion.20 = f32[1024,8,128]{2,0,1:T(8,128)S(1)} fusion(f32[1,1,1024,8,128]{4,2,3,1,0:T(8,128)} %copy.70, f32[1,1,1024,8,128]{4,2,3,1,0:T(8,128)} %copy.69, f32[1,1,1024,8,128]{4,2,3,1,0:T(8,128)} %copy.68, f32[]{:T(128)} %fusion.66, s32[384]{0:T(512)S(1)} %iota_add_fusion.1), kind=kOutput, calls=%fused_computation.23 | convolution fusion | flops 4838621184 | bytes 16778756 | tf_op jit(solution)/shard_map/mnrjk,nko->mrjo/dot_general | solution.py:82
  394.4 2.0 copy-done
  396.4 1.9 collective-permute-start
  398.6 4.5 %collective-permute-start.1 = (f32[15,1024]{0,1:T(8,128)S(1)}, f32[15,1024]{0,1:T(8,128)S(1)}, u32[]{:S(2)}, u32[]{:S(2)}) collective-permute-start(f32[15,1024]{0,1:T(8,128)S(1)} %bitcast.89), channel_id=1, source_target_pairs={{4,0},{8,4},{12,8},{16,12},{20,16},{24,20},{28,24},{5,1},{9,5},{13... | collective-permute-start | bytes 184328 | tf_op jit(solution)/shard_map/ppermute | solution.py:26
  403.1 2.9 divide_select_fusion
  406.0 1.1 constant_dynamic-slice_fusion
  407.1 5.3 %copy.56 = f32[1024,8,128]{0,2,1:T(8,128)} copy(f32[1024,8,128]{2,0,1:T(8,128)} %copy-done) | data formatting | bytes 8388608 | tf_op jit(solution)/shard_map/mnrjk,nko->mrjo/dot_general | solution.py:82
  412.7 6.4 %concatenate.13 = f32[1054,1024]{0,1:T(8,128)} concatenate(f32[15,1024]{0,1:T(8,128)S(1)} %copy.59, f32[1024,1024]{0,1:T(8,128)} %bitcast.86, f32[15,1024]{0,1:T(8,128)S(1)} %collective-permute-done.1), dimensions={0} | concatenate | bytes 8634368 | tf_op jit(solution)/shard_map/concatenate | solution.py:22
  419.1 5.4 %fusion.26 = f32[256,1024]{1,0:T(8,128)} fusion(f32[1054,1024]{0,1:T(8,128)} %concatenate.13, s32[]{:T(128)S(6)} %select_n.209, f32[]{:T(128)} %fusion.66, s32[286]{0:T(512)S(1)} %iota_add_fusion), kind=kOutput, calls=%fused_computation.32 | convolution fusion | flops 900410368 | bytes 2623100 | tf_op jit(solution)/shard_map/dot_general | solution.py:160
  (47 shorter events, 4.8 us)
Async XLA Ops:
  11.2 118.2 %all-to-all-start = ((f32[8,1,512]{2,1,0:T(1,128)}), f32[8,1,512]{2,1,0:T(1,128)S(1)}, u32[]{:S(2)}, u32[]{:S(2)}) async-start(f32[8,1,512]{2,1,0:T(1,128)} %reshape.484), calls=%async_computation | async-start | bytes 32768 | tf_op jit(solution)/shard_map/all_to_all | solution.py:142
  129.4 52.2 %all-to-all-start.1 = ((f32[8,8,16,1024]{3,1,2,0:T(8,128)}), f32[8,8,16,1024]{3,1,2,0:T(8,128)}, u32[]{:S(2)}, u32[]{:S(2)}) async-start(f32[8,8,16,1024]{3,1,2,0:T(8,128)} %fusion.25), calls=%async_computation.1 | async-start | bytes 8388608 | tf_op jit(solution)/shard_map/all_to_all | solution.py:141
  133.9 213.4 %all-reduce.4.cloned.1.call-start = ((), (), s32[]{:S(2)}) async-start(), calls=%async_computation.2 | async-start | bytes 8388608 | tf_op jit(solution)/shard_map/psum | solution.py:151
  394.3 2.0 copy-start
  396.4 16.0 %collective-permute-start = (f32[15,1024]{1,0:T(8,128)S(1)}, f32[15,1024]{1,0:T(8,128)S(1)}, u32[]{:S(2)}, u32[]{:S(2)}) collective-permute-start(f32[15,1024]{1,0:T(8,128)S(1)} %bitcast.92), channel_id=1, source_target_pairs={{0,4},{4,8},{8,12},{12,16},{16,20},{20,24},{24,28},{1,5},{5,9},{9,... | collective-permute-start | bytes 184328 | tf_op jit(solution)/shard_map/ppermute | solution.py:24
  398.6 14.1 %collective-permute-start.1 = (f32[15,1024]{0,1:T(8,128)S(1)}, f32[15,1024]{0,1:T(8,128)S(1)}, u32[]{:S(2)}, u32[]{:S(2)}) collective-permute-start(f32[15,1024]{0,1:T(8,128)S(1)} %bitcast.89), channel_id=1, source_target_pairs={{4,0},{8,4},{12,8},{16,12},{20,16},{24,20},{28,24},{5,1},{9,5},{13... | collective-permute-start | bytes 184328 | tf_op jit(solution)/shard_map/ppermute | solution.py:26
Sparse Core Ops, SparseCore 0:
  191.9 155.3 all-reduce.3
where the time goes:
time: 433 us; the launch traced here: 431 us
  waiting for transfers between devices  189 us (44%)
  local copies, waits for them, and re-layouts  92.3 us (21%)
  matrix products  81.7 us (19%)
  other arithmetic  22.7 us (5%)
  between operations  18.2 us (4%)
  starting transfers between devices  15.2 us (4%)
  blocking collectives  12.2 us (3%)
    psum x1, waiting for transfers between devices, shards(): summed_image, weight_sums = lax.psum((numerator, weight_total), 'vis')  142 us
    all_to_all x1, waiting for transfers between devices, shards(): lax.all_to_all(sent_images, 'tile', split_axis=0, concat_axis=0, tiled=True)  46.4 us
    dot_general x5, matrix products, column_pass(): result = jnp.einsum('mnrjk,nko->mrjo', framed, windows, precision=highest)  34.5 us
    unnamed x11, local copies, waits for them, and re-layouts  24.9 us
    slice x5, local copies, waits for them, and re-layouts, column_pass(): viewed[:, :, :, 0:blocks]  24.7 us
    dot_general x4, matrix products, match_pieces(): mixed = jnp.einsum('mab,maqc->mbqc', factors, rowed, precision=highest)  20.7 us
    dot_general x4, matrix products, match_pieces(): rowed = jnp.einsum('aqp,mpc->maqc', row_bank, images, precision=highest)  15.3 us
    psum x1, blocking collectives, shards(): summed_image, weight_sums = lax.psum((numerator, weight_total), 'vis')  12.2 us
  transfers between devices with their start and end apart: 5, of which 2 were waited for; matrix products, arithmetic and copies ran while one was open for 28% of the time, Pallas kernels for 0%

commit v1 on v0

v1 whole, which is shorter than its diff:
```python
import functools

import jax
import jax.numpy as jnp
import ml_dtypes
import numpy as np
from jax import lax
from jax.experimental import pallas as pl
from jax.experimental.pallas import tpu as pltpu
from jax.sharding import PartitionSpec as P

SR = 1024
TAPS = 10
REACH = 15
LANES = 128
SIDE = 64
RIM = 16
GROUP = 4

row_shapes = ((1.0, 0), (1.0, 1), (2.0, 0), (2.0, 2), (3.5, 0))
column_shapes = ((1.0, 0), (2.0, 0), (2.0, 1), (3.5, 0))
highest = lax.Precision.HIGHEST
F32 = jnp.float32
BF16 = jnp.bfloat16


def shaped_taps(lags, shapes, reach):
    spots = np.arange(-reach, reach + 1).astype(np.float64)
    lags = lags.astype(np.float64)
    stacked = []
    for spread, degree in shapes:
        full = np.exp(-spots * spots / (2.0 * spread * spread)) * (spots / spread) ** degree
        values = np.exp(-lags * lags / (2.0 * spread * spread)) * (lags / spread) ** degree
        values = values / np.sqrt(np.sum(full * full))
        stacked.append(np.where(np.abs(lags) <= reach, values, 0.0))
    return np.stack(stacked)


def detect_taps(lags, reach):
    spots = np.arange(-reach, reach + 1).astype(np.float64)
    total = np.sum(np.exp(-spots * spots / 18.0))
    lags = lags.astype(np.float64)
    values = np.exp(-lags * lags / 18.0) / total - 1.0 / (2 * reach + 1)
    return np.where(np.abs(lags) <= reach, values, 0.0)


def halves_np(table):
    table = table.astype(np.float32)
    top = table.astype(ml_dtypes.bfloat16)
    rest = (table - top.astype(np.float32)).astype(ml_dtypes.bfloat16)
    return jnp.asarray(top), jnp.asarray(rest)


def halves(x):
    top = x.astype(BF16)
    return top, (x - top.astype(F32)).astype(BF16)


def dot(a, b):
    return jnp.dot(a, b, preferred_element_type=F32)


def window_lags():
    return np.arange(2 * SIDE + LANES)[:, None] - SIDE - np.arange(LANES)[None, :]


def windows_of(x):
    rows, width = x.shape
    rim = jnp.zeros((rows, SIDE), x.dtype)
    padded = jnp.concatenate([rim, x, rim], axis=1)
    blocks = width // LANES
    return jnp.concatenate(
        [padded[:, LANES * j : LANES * (j + 2)] for j in range(blocks)], axis=0
    )


def match_body(capacity, routes_ref, pieces_ref, mix_ref, top_ref, rest_ref, out_ref, count_ref):
    step = pl.program_id(0)
    pieces, rows, width = pieces_ref.shape
    kinds = top_ref.shape[1] // LANES
    blocks = width // LANES

    @pl.when(step == 0)
    def _():
        out_ref[...] = jnp.zeros_like(out_ref)

        @pl.loop(0, count_ref.shape[0])
        def _(i):
            count_ref[i] = 0

    flat = pieces_ref[...].reshape(pieces * rows, width)
    wide = windows_of(flat)
    top, rest = halves(wide)
    swept = dot(top, top_ref[...]) + (dot(rest, top_ref[...]) + dot(top, rest_ref[...]))
    span = GROUP * rows
    for q in range(pieces // GROUP):
        parts = []
        for j in range(blocks):
            at = j * pieces * rows + q * span
            parts.append(
                jnp.concatenate(
                    [swept[at : at + span, LANES * b : LANES * (b + 1)] for b in range(kinds)],
                    axis=0,
                )
            )
        banked = jnp.concatenate(parts, axis=1)
        y_top, y_rest = halves(banked)
        m_top, m_rest = halves(mix_ref[q])
        result = dot(m_top, y_top) + (dot(m_rest, y_top) + dot(m_top, y_rest))
        for i in range(GROUP):
            strip = routes_ref[step * pieces + q * GROUP + i]
            rank = count_ref[strip]
            count_ref[strip] = rank + 1
            out_ref[strip * capacity + rank] = result[i * rows : (i + 1) * rows]


def match(pieces, mix, routes, tiles, capacity):
    count, rows, width = pieces.shape
    batch = 8
    top, rest = halves_np(
        np.concatenate(list(shaped_taps(window_lags(), column_shapes, TAPS)), axis=1)
    )
    groups = batch // GROUP
    return pl.pallas_call(
        functools.partial(match_body, capacity),
        grid_spec=pltpu.PrefetchScalarGridSpec(
            num_scalar_prefetch=1,
            grid=(count // batch,),
            in_specs=[
                pl.BlockSpec((batch, rows, width), lambda i, r: (i, 0, 0)),
                pl.BlockSpec((groups,) + mix.shape[1:], lambda i, r: (i, 0, 0)),
                pl.BlockSpec(top.shape, lambda i, r: (0, 0)),
                pl.BlockSpec(rest.shape, lambda i, r: (0, 0)),
            ],
            out_specs=pl.BlockSpec((tiles * capacity, rows, width), lambda i, r: (0, 0, 0)),
            scratch_shapes=[pltpu.SMEM((tiles,), jnp.int32)],
        ),
        out_shape=jax.ShapeDtypeStruct((tiles * capacity, rows, width), F32),
        compiler_params=pltpu.CompilerParams(vmem_limit_bytes=50 * 2**20),
        name="match",
    )(routes, pieces, mix, top, rest)


def mix_table(coeffs, weights, rows):
    count, kinds_row, kinds = coeffs.shape
    lag = np.arange(rows)[None, :] - np.arange(rows)[:, None]
    bank = jnp.asarray(shaped_taps(lag, row_shapes, TAPS).astype(np.float32))
    weighted = coeffs * weights[:, None, None]
    each = jnp.einsum("mab,aqp->mqbp", weighted, bank, precision=highest)
    each = each.reshape(count // GROUP, GROUP, rows, kinds, 1, rows)
    same = np.eye(GROUP, dtype=bool)[None, :, None, None, :, None]
    return jnp.where(same, each, 0.0).reshape(
        count // GROUP, GROUP * rows, kinds * GROUP * rows
    )


def gather_body(spot_ref, landed_ref, out_ref):
    out_ref[...] = jnp.zeros_like(out_ref)

    @pl.loop(0, landed_ref.shape[0])
    def _(i):
        out_ref[spot_ref[i]] += landed_ref[i]


def scatter_add(landed, spots, blocks):
    slots, rows, width = landed.shape
    return pl.pallas_call(
        gather_body,
        grid_spec=pltpu.PrefetchScalarGridSpec(
            num_scalar_prefetch=1,
            grid=(1,),
            in_specs=[pl.BlockSpec(landed.shape, lambda i, r: (0, 0, 0))],
            out_specs=pl.BlockSpec((blocks, rows, width), lambda i, r: (0, 0, 0)),
        ),
        out_shape=jax.ShapeDtypeStruct((blocks, rows, width), F32),
        compiler_params=pltpu.CompilerParams(vmem_limit_bytes=50 * 2**20),
        name="scatter_add",
    )(spots, landed)


def detect_body(above_ref, here_ref, below_ref, top_ref, rest_ref, band_top_ref, band_rest_ref, out_ref):
    cells = jnp.concatenate([above_ref[...], here_ref[...], below_ref[...]], axis=0)
    rows, width = cells.shape
    top, rest = halves(windows_of(cells))
    swept = dot(top, top_ref[...]) + (dot(rest, top_ref[...]) + dot(top, rest_ref[...]))
    sheet = jnp.concatenate(
        [swept[j * rows : (j + 1) * rows] for j in range(width // LANES)], axis=1
    )
    s_top, s_rest = halves(sheet)
    b_top, b_rest = band_top_ref[...], band_rest_ref[...]
    out_ref[...] = dot(b_top, s_top) + (dot(b_rest, s_top) + dot(b_top, s_rest))


def detect(above, here, below):
    rows = here.shape[0]
    top, rest = halves_np(detect_taps(window_lags(), REACH))
    lag = np.arange(rows + 2 * RIM)[None, :] - RIM - np.arange(rows)[:, None]
    band_top, band_rest = halves_np(detect_taps(lag, REACH))
    return pl.pallas_call(
        detect_body,
        out_shape=jax.ShapeDtypeStruct(here.shape, F32),
        compiler_params=pltpu.CompilerParams(vmem_limit_bytes=50 * 2**20),
        name="detect",
    )(above, here, below, top, rest, band_top, band_rest)


def shards(pieces, coeffs, weights, routes, offsets):
    tiles, quarters = lax.axis_size("tile"), lax.axis_size("vis")
    me_tile, me_vis = lax.axis_index("tile"), lax.axis_index("vis")
    count, rows, width = pieces.shape
    capacity = max(2, 2 * count // tiles)
    blocks = SR // rows
    target = routes[:, 0]
    facts = jnp.stack([target.astype(F32), offsets.astype(F32), weights])
    known = lax.all_gather(facts, ("tile", "vis"))
    sent = match(pieces, mix_table(coeffs, weights, rows), target, tiles, capacity)
    sent = sent.reshape(tiles, capacity, rows, width)
    landed = lax.all_to_all(sent, "tile", split_axis=0, concat_axis=0, tiled=True)
    landed = landed.reshape(tiles * capacity, rows, width)
    mine = known[:, 0] == me_tile.astype(F32)
    grid_of = jnp.arange(blocks).astype(F32)
    near_vis = lax.dynamic_slice_in_dim(
        known.reshape(tiles, quarters, 3, count), me_vis, 1, 1
    )[:, 0]
    hit = near_vis[:, 0] == me_tile.astype(F32)
    earlier = np.arange(count)[None, :] < np.arange(count)[:, None]
    rank = jnp.sum(jnp.where(earlier[None] & hit[:, None, :], 1, 0), axis=2)
    slot_hit = hit[:, None, :] & (rank[:, None, :] == jnp.arange(capacity)[None, :, None])
    spots = jnp.sum(jnp.where(slot_hit, near_vis[:, None, 1], 0.0), axis=2)
    spots = spots.astype(jnp.int32).reshape(-1)
    own_blocks = blocks // quarters
    own_grid = (me_vis * own_blocks + jnp.arange(own_blocks)).astype(F32)
    on_block = mine[None] & (known[:, 1][None] == own_grid[:, None, None])
    masses = jnp.sum(jnp.where(on_block, known[:, 2][None], 0.0), axis=(1, 2))
    inverse = jnp.where(masses > 0.0, 1.0 / jnp.where(masses > 0.0, masses, 1.0), 0.0)
    numerator = scatter_add(landed, spots, blocks)
    summed = lax.psum_scatter(numerator, "vis", scatter_dimension=0, tiled=True)
    coadd = jnp.where(
        (masses > 0.0)[:, None, None], summed * inverse[:, None, None], 0.0
    ).reshape(own_blocks * rows, width)
    total = tiles * quarters
    both = ("tile", "vis")
    above = lax.ppermute(coadd[-RIM:], both, [(i, i + 1) for i in range(total - 1)])
    below = lax.ppermute(coadd[:RIM], both, [(i + 1, i) for i in range(total - 1)])
    return coadd, detect(above, coadd, below)


def solution(mesh):
    placed = (
        P(("tile", "vis"), None, None),
        P(("tile", "vis"), None, None),
        P(("tile", "vis")),
        P(("tile", "vis"), None),
        P(("tile", "vis")),
    )
    return jax.shard_map(
        shards,
        mesh=mesh,
        in_specs=placed,
        out_specs=(P(("tile", "vis"), None), P(("tile", "vis"), None)),
        check_vma=False,
    )
```

time: 433 us -> 211 us (0.49)
  waiting for transfers between devices: 189 us -> 81 us
  local copies, waits for them, and re-layouts: 92.3 us -> 10.8 us
  matrix products: 81.7 us -> 1.48 us
  blocking collectives: 12.2 us -> 69.6 us
  other arithmetic: 22.7 us -> 2.8 us
  Pallas kernels: 0 us -> 19.3 us
    psum x1 -> x0, waiting for transfers between devices: 142 us -> none  [shards(): summed_image, weight_sums = lax.psum((numerator, weight_total), 'vis')]
    dot_general x15 -> x1, matrix products: 81.7 us -> 1.48 us  [mix_table(): each = jnp.einsum('mab,aqp->mqbp', weighted, bank, precision=highest)]
    reduce_scatter x0 -> x1, waiting for transfers between devices: none -> 73.8 us  [shards(): summed = lax.psum_scatter(numerator, 'vis', scatter_dimension=0, tiled=True)]
    all_gather x0 -> x1, blocking collectives: none -> 69.6 us  [shards(): known = lax.all_gather(facts, ('tile', 'vis'))]
    all_to_all x2 -> x1, waiting for transfers between devices: 46.4 us -> 0.01 us  [shards(): lax.all_to_all(sent, 'tile', split_axis=0, concat_axis=0, tiled=True)]
    slice x8 -> x2, local copies, waits for them, and re-layouts: 25 us -> 0.05 us  [the longest x1 0.04 us: shards(): mine = known[:, 0] == me_tile.astype(F32)]
    unnamed x11 -> x25, local copies, waits for them, and re-layouts: 24.9 us -> 0.05 us
    pallas_call x0 -> x3, Pallas kernels: none -> 19.3 us  [the longest x1 9.4 us: match(): pl.pallas_call(functools.partial(match_body, capacity), grid_spec=pltpu.P...]
  transfers between devices with their start and end apart: 5 -> 4, of which waited for: 2 -> 2; matrix products, arithmetic and copies ran while one was open for 28% -> 0% of each run, Pallas kernels for 0% -> 0%
where the time goes in v1:
time: 211 us
  waiting for transfers between devices  81 us (38%)
  blocking collectives  69.6 us (33%)
  Pallas kernels  19.3 us (9%)
  between operations  14.3 us (7%)
  starting transfers between devices  11.7 us (6%)
  local copies, waits for them, and re-layouts  10.8 us (5%)
  other arithmetic  2.8 us (1%)
    reduce_scatter x1, waiting for transfers between devices, shards(): summed = lax.psum_scatter(numerator, 'vis', scatter_dimension=0, tiled=True)  73.8 us
    all_gather x1, blocking collectives, shards(): known = lax.all_gather(facts, ('tile', 'vis'))  69.6 us
    broadcast_in_dim x5, local copies, waits for them, and re-layouts, mix_table(): jnp.where(same, each, 0.0)  9.66 us
    pallas_call x1, Pallas kernels, match(): pl.pallas_call(functools.partial(match_body, capacity), grid_spec=pltpu.P...  9.4 us
    ppermute x1, waiting for transfers between devices, shards(): lax.ppermute(coadd[-RIM:], both, [(i, i + 1) for i in range(total - 1)])  7.24 us
    pallas_call x1, Pallas kernels, scatter_add(): pl.pallas_call(gather_body, grid_spec=pltpu.PrefetchScalarGridSpec(num_sc...  5.65 us
    ppermute x1, starting transfers between devices, shards(): lax.ppermute(coadd[:RIM], both, [(i + 1, i) for i in range(total - 1)])  5.13 us
    all_to_all x1, starting transfers between devices, shards(): lax.all_to_all(sent, 'tile', split_axis=0, concat_axis=0, tiled=True)  4.64 us
  transfers between devices with their start and end apart: 4, of which 2 were waited for; matrix products, arithmetic and copies ran while one was open for 0% of the time, Pallas kernels for 0%

profile of v1, /device:TPU:4, one launch (start us, length us, event | category | flops | bytes accessed | tf_op | source)
XLA Modules:
  0.0 211.0 jit_solution(17747516206636055358)
XLA Ops:
  7.2 0.8 broadcast_in_dim.100
  8.0 0.3 broadcast_in_dim.101
  8.2 0.7 multiply_bitcast_fusion
  8.9 1.5 convolution_bitcast_fusion
  10.4 0.9 copy.30
  11.4 0.4 copy.31
  11.8 2.7 %broadcast_in_dim.104 = f32[8,4,16,4,4,16]{5,4,3,2,1,0:T(4,128)} broadcast(f32[8,4,16,4,16]{4,3,2,1,0:T(4,128)S(1)} %copy.31), dimensions={0,1,2,3,5} | broadcast | bytes 655360 | tf_op jit(solution)/shard_map/jit(_where)/broadcast_in_dim | solution.py:152
  14.5 0.0 copy-start.1
  14.5 0.0 copy-start.2
  14.5 0.0 copy-start.3
  14.5 0.0 copy-start.8
  14.5 5.4 %broadcast_in_dim.105 = f32[8,64,256]{2,1,0:T(8,128)S(1)} reshape(f32[8,4,16,4,4,16]{5,4,3,2,1,0:T(4,128)} %broadcast_in_dim.104) | data formatting | bytes 1048576 | tf_op jit(solution)/shard_map/jit(_where)/broadcast_in_dim | solution.py:152
  20.0 0.0 copy-done.1
  20.0 0.0 copy-done.2
  20.0 0.0 copy-done.3
  20.0 0.0 copy-done.8
  20.1 9.4 %match.1 = f32[64,16,1024]{2,1,0:T(8,128)} custom-call(s32[32]{0:T(128)S(1)} %bitcast.38, f32[32,16,1024]{2,1,0:T(8,128)S(1)} %copy-done.1, f32[8,64,256]{2,1,0:T(8,128)S(1)} %broadcast_select_fusion.mix_ref, bf16[256,512]{1,0:T(8,128)(2,1)S(1)} %copy-done.3, bf16[256,512]{1,0:T(8,128)(2,1)S(1)} %copy-done.2), custom_call_target="tpu_custom_call" | custom-call | tf_op jit(solution)/shard_map/match/pallas_call | solution.py:124
  29.5 0.0 copy-start.11
  29.5 0.0 copy-start.10
  29.5 0.0 copy-start.9
  29.5 4.6 %all-to-all-start = ((f32[8,8,16,1024]{3,2,1,0:T(8,128)}), f32[8,8,16,1024]{3,2,1,0:T(8,128)}, u32[]{:S(2)}, u32[]{:S(2)}) async-start(f32[8,8,16,1024]{3,2,1,0:T(8,128)} %bitcast.39), calls=%async_computation | async-start | bytes 8388608 | tf_op jit(solution)/shard_map/all_to_all | solution.py:218
  34.1 0.0 reduce-scatter.2.cloned.1.call-start
  34.2 0.0 copy-done.11
  34.2 0.0 copy-done.10
  34.2 69.6 %all-gather.1 = f32[32,3,32]{2,1,0:T(4,128)S(1)} all-gather(f32[1,3,32]{2,1,0:T(4,128)S(1)} %maximum_bitcast_fusion), channel_id=2, replica_groups=mesh['tile'=8,'vis'=4] {'tile','vis'}, dimensions={0}, use_global_device_ids=true | all-gather | bytes 12672 | tf_op jit(solution)/shard_map/all_gather | solution.py:215
  103.9 0.0 copy-done.9
  103.9 0.2 select_reduce_fusion.1
  104.1 0.1 select_reduce_fusion.2
  104.2 0.1 convert_element_type.40.spot_ref
  104.3 0.0 all-to-all-done
  104.3 5.6 %scatter_add.1 = f32[64,16,1024]{2,1,0:T(8,128)} custom-call(s32[64]{0:T(128)S(1)} %convert_element_type.40.spot_ref, f32[64,16,1024]{2,1,0:T(8,128)} %bitcast.17.landed_ref), custom_call_target="tpu_custom_call" | custom-call | tf_op jit(solution)/shard_map/scatter_add/pallas_call | solution.py:167
  110.0 0.0 copy-start.4
  110.0 0.0 copy-start.5
  110.0 0.0 copy-start.6
  110.0 0.0 copy-start.7
  110.0 0.0 reduce-scatter.2.cloned.1.call-update
  110.1 0.3 select_reduce_fusion
  110.4 73.8 %reduce-scatter.2.cloned.1.call-done = f32[16,16,1024]{2,1,0:T(8,128)} async-done(((f32[64,16,1024]{2,1,0:T(8,128)}), f32[16,16,1024]{2,1,0:T(8,128)}) %reduce-scatter.2.cloned.1.call-update) | async-done | bytes 1048592 | tf_op jit(solution)/shard_map/reduce_scatter | solution.py:237
  184.1 1.4 multiply_select_fusion
  185.5 0.0 copy-start
  185.6 5.1 %collective-permute-start.1 = (f32[16,1024]{1,0:T(8,128)S(1)}, f32[16,1024]{1,0:T(8,128)S(1)}, u32[]{:S(2)}, u32[]{:S(2)}) collective-permute-start(f32[16,1024]{1,0:T(8,128)S(1)} %get-tuple-element.2), channel_id=1, source_target_pairs={{1,0},{2,1},{3,2},{4,3},{5,4},{6,5},{7,6},{8,7},{9,8},{10,9},{11,1... | collective-permute-start | bytes 196616 | tf_op jit(solution)/shard_map/ppermute | solution.py:244
  190.7 1.9 collective-permute-start
  192.6 0.0 collective-permute-done.1.below_ref
  192.6 7.2 %collective-permute-done.above_ref = f32[16,1024]{1,0:T(8,128)S(1)} collective-permute-done((f32[16,1024]{1,0:T(8,128)S(1)}, f32[16,1024]{1,0:T(8,128)S(1)}, u32[]{:S(2)}, u32[]{:S(2)}) %collective-permute-start) | collective-permute-done | bytes 65568 | tf_op jit(solution)/shard_map/ppermute | solution.py:243
  199.9 0.0 copy-done.4
  199.9 0.0 copy-done.5
  199.9 0.0 copy-done.6
  199.9 0.0 copy-done.7
  199.9 4.2 %detect.1 = f32[256,1024]{1,0:T(8,128)} custom-call(f32[16,1024]{1,0:T(8,128)S(1)} %collective-permute-done.above_ref, f32[256,1024]{1,0:T(8,128)S(1)} %bitcast.36, f32[16,1024]{1,0:T(8,128)S(1)} %collective-permute-done.1.below_ref, bf16[256,128]{1,0:T(8,128)(2,1)S(1)} %copy-done.7, bf16[256,128]{1,0:T(8,128)(2,1)S(1)} %copy-done.6, ...), custom_call_target="tpu_custom_call" | custom-call | tf_op jit(solution)/shard_map/detect/pallas_call | solution.py:199
  204.1 0.0 copy-done
  (15 shorter events, 0.2 us)
Async XLA Ops:
  14.5 5.5 %copy-start.1 = (f32[32,16,1024]{2,1,0:T(8,128)S(1)}, f32[32,16,1024]{2,1,0:T(8,128)}, u32[]{:S(2)}) copy-start(f32[32,16,1024]{2,1,0:T(8,128)} %pieces_ref.1) | copy-start | bytes 6291460
  14.5 5.5 %copy-start.2 = (bf16[256,512]{1,0:T(8,128)(2,1)S(1)}, bf16[256,512]{1,0:T(8,128)(2,1)}, u32[]{:S(2)}) copy-start(bf16[256,512]{1,0:T(8,128)(2,1)} %constant.44.clone.rest_ref) | copy-start | bytes 786436
  14.5 5.5 %copy-start.3 = (bf16[256,512]{1,0:T(8,128)(2,1)S(1)}, bf16[256,512]{1,0:T(8,128)(2,1)}, u32[]{:S(2)}) copy-start(bf16[256,512]{1,0:T(8,128)(2,1)} %constant.43.clone.top_ref) | copy-start | bytes 786436
  14.5 5.5 %copy-start.8 = (s32[32,1]{0,1:T(1,128)S(1)}, s32[32,1]{0,1:T(1,128)}, u32[]{:S(2)}) copy-start(s32[32,1]{0,1:T(1,128)} %param.17) | copy-start | bytes 388
  29.5 4.7 %copy-start.11 = (s32[32]{0:T(128)S(1)}, s32[32]{0:T(128)}, u32[]{:S(2)}) copy-start(s32[32]{0:T(128)} %param.18) | copy-start | bytes 388
  29.5 4.7 %copy-start.10 = (f32[32]{0:T(128)S(1)}, f32[32]{0:T(128)}, u32[]{:S(2)}) copy-start(f32[32]{0:T(128)} %param.16) | copy-start | bytes 388
  29.5 74.4 %copy-start.9 = (pred[32,32]{1,0:T(32,128)(4,1)S(1)}, pred[32,32]{1,0:T(32,128)(4,1)}, u32[]{:S(2)}) copy-start(pred[32,32]{1,0:T(32,128)(4,1)} %constant.50) | copy-start | bytes 3076
  29.5 74.8 %all-to-all-start = ((f32[8,8,16,1024]{3,2,1,0:T(8,128)}), f32[8,8,16,1024]{3,2,1,0:T(8,128)}, u32[]{:S(2)}, u32[]{:S(2)}) async-start(f32[8,8,16,1024]{3,2,1,0:T(8,128)} %bitcast.39), calls=%async_computation | async-start | bytes 8388608 | tf_op jit(solution)/shard_map/all_to_all | solution.py:218
  34.1 150.0 %reduce-scatter.2.cloned.1.call-start = ((), (), s32[]{:S(2)}) async-start(), calls=%async_computation.2 | async-start | bytes 5242880 | tf_op jit(solution)/shard_map/reduce_scatter | solution.py:237
  110.0 89.9 %copy-start.4 = (bf16[256,288]{1,0:T(8,128)(2,1)S(1)}, bf16[256,288]{1,0:T(8,128)(2,1)}, u32[]{:S(2)}) copy-start(bf16[256,288]{1,0:T(8,128)(2,1)} %constant.49.clone.band_rest_ref) | copy-start | bytes 442372
  110.0 89.9 %copy-start.5 = (bf16[256,288]{1,0:T(8,128)(2,1)S(1)}, bf16[256,288]{1,0:T(8,128)(2,1)}, u32[]{:S(2)}) copy-start(bf16[256,288]{1,0:T(8,128)(2,1)} %constant.48.clone.band_top_ref) | copy-start | bytes 442372
  110.0 89.9 %copy-start.6 = (bf16[256,128]{1,0:T(8,128)(2,1)S(1)}, bf16[256,128]{1,0:T(8,128)(2,1)}, u32[]{:S(2)}) copy-start(bf16[256,128]{1,0:T(8,128)(2,1)} %constant.47.clone.rest_ref) | copy-start | bytes 196612
  110.0 89.9 %copy-start.7 = (bf16[256,128]{1,0:T(8,128)(2,1)S(1)}, bf16[256,128]{1,0:T(8,128)(2,1)}, u32[]{:S(2)}) copy-start(bf16[256,128]{1,0:T(8,128)(2,1)} %constant.46.clone.top_ref) | copy-start | bytes 196612
  185.5 18.6 %copy-start = (f32[16,16,1024]{2,1,0:T(8,128)}, f32[16,16,1024]{2,1,0:T(8,128)S(1)}, u32[]{:S(2)}) copy-start(f32[16,16,1024]{2,1,0:T(8,128)S(1)} %multiply_select_fusion) | copy-start | bytes 3145732
  185.6 7.1 %collective-permute-start.1 = (f32[16,1024]{1,0:T(8,128)S(1)}, f32[16,1024]{1,0:T(8,128)S(1)}, u32[]{:S(2)}, u32[]{:S(2)}) collective-permute-start(f32[16,1024]{1,0:T(8,128)S(1)} %get-tuple-element.2), channel_id=1, source_target_pairs={{1,0},{2,1},{3,2},{4,3},{5,4},{6,5},{7,6},{8,7},{9,8},{10,9},{11,1... | collective-permute-start | bytes 196616 | tf_op jit(solution)/shard_map/ppermute | solution.py:244
  190.7 9.2 %collective-permute-start = (f32[16,1024]{1,0:T(8,128)S(1)}, f32[16,1024]{1,0:T(8,128)S(1)}, u32[]{:S(2)}, u32[]{:S(2)}) collective-permute-start(f32[16,1024]{1,0:T(8,128)S(1)} %get-tuple-element.3), channel_id=1, source_target_pairs={{0,1},{1,2},{2,3},{3,4},{4,5},{5,6},{6,7},{7,8},{8,9},{9,10},{10,1... | collective-permute-start | bytes 196616 | tf_op jit(solution)/shard_map/ppermute | solution.py:243
Sparse Core Ops, SparseCore 0:
  110.1 73.9 reduce-scatter.1

commit v2 on v1

--- a/solution.py
+++ b/solution.py
@@ -16,6 +16,7 @@
 SIDE = 64
 RIM = 16
 GROUP = 4
+CHUNK = 256
 
 row_shapes = ((1.0, 0), (1.0, 1), (2.0, 0), (2.0, 2), (3.5, 0))
 column_shapes = ((1.0, 0), (2.0, 0), (2.0, 1), (3.5, 0))
@@ -111,7 +112,10 @@
             strip = routes_ref[step * pieces + q * GROUP + i]
             rank = count_ref[strip]
             count_ref[strip] = rank + 1
-            out_ref[strip * capacity + rank] = result[i * rows : (i + 1) * rows]
+            for c in range(out_ref.shape[0]):
+                out_ref[c, strip * capacity + rank] = result[
+                    i * rows : (i + 1) * rows, c * CHUNK : (c + 1) * CHUNK
+                ]
 
 
 def match(pieces, mix, routes, tiles, capacity):
@@ -121,6 +125,7 @@
         np.concatenate(list(shaped_taps(window_lags(), column_shapes, TAPS)), axis=1)
     )
     groups = batch // GROUP
+    shape = (width // CHUNK, tiles * capacity, rows, CHUNK)
     return pl.pallas_call(
         functools.partial(match_body, capacity),
         grid_spec=pltpu.PrefetchScalarGridSpec(
@@ -132,10 +137,10 @@
                 pl.BlockSpec(top.shape, lambda i, r: (0, 0)),
                 pl.BlockSpec(rest.shape, lambda i, r: (0, 0)),
             ],
-            out_specs=pl.BlockSpec((tiles * capacity, rows, width), lambda i, r: (0, 0, 0)),
+            out_specs=pl.BlockSpec(shape, lambda i, r: (0, 0, 0, 0)),
             scratch_shapes=[pltpu.SMEM((tiles,), jnp.int32)],
         ),
-        out_shape=jax.ShapeDtypeStruct((tiles * capacity, rows, width), F32),
+        out_shape=jax.ShapeDtypeStruct(shape, F32),
         compiler_params=pltpu.CompilerParams(vmem_limit_bytes=50 * 2**20),
         name="match",
     )(routes, pieces, mix, top, rest)
@@ -154,54 +159,267 @@
     )
 
 
-def gather_body(spot_ref, landed_ref, out_ref):
-    out_ref[...] = jnp.zeros_like(out_ref)
-
-    @pl.loop(0, landed_ref.shape[0])
-    def _(i):
-        out_ref[spot_ref[i]] += landed_ref[i]
-
-
-def scatter_add(landed, spots, blocks):
-    slots, rows, width = landed.shape
+def combine_body(
+    tiles, quarters, spot_ref, inverse_ref, sent_ref, top_ref, rest_ref, band_top_ref, band_rest_ref,
+    coadd_ref, out_ref,
+    landed, select, part, right, left, sheet,
+    ring_send, ring_recv, right_send, right_recv, left_send, left_recv, rim_send, rim_recv,
+):
+    tile, vis = lax.axis_index("tile"), lax.axis_index("vis")
+    chunks, _, span, chunk = landed.shape
+    slots = tiles * span
+    strip = select.shape[0]
+    own = strip // quarters
+    first, last = vis == 0, vis == quarters - 1
+    down = (
+        lax.select(first, tile - 1, tile),
+        lax.select(first, quarters - 1, vis - 1),
+    )
+    up = (lax.select(last, tile + 1, tile), lax.select(last, 0, vis + 1))
+    has_down = jnp.logical_or(tile > 0, vis > 0)
+    has_up = jnp.logical_or(tile < tiles - 1, vis < quarters - 1)
+
+    barrier = pltpu.get_barrier_semaphore()
+
+    def greet(device):
+        pl.semaphore_signal(barrier, inc=1, device_id=device, device_id_type=pl.DeviceIdType.MESH)
+
+    @pl.loop(1, tiles)
+    def _(k):
+        greet((lax.rem(tile + k, tiles), vis))
+
+    @pl.when(has_down)
+    def _():
+        greet(down)
+
+    @pl.when(has_up)
+    def _():
+        greet(up)
+
+    pl.semaphore_wait(
+        barrier, tiles - 1 + has_down.astype(jnp.int32) + has_up.astype(jnp.int32)
+    )
+
+    def ring(c, k):
+        peer = lax.rem(tile + k, tiles)
+        return pltpu.make_async_remote_copy(
+            src_ref=sent_ref.at[c, peer],
+            dst_ref=landed.at[c, tile],
+            send_sem=ring_send.at[c, k],
+            recv_sem=ring_recv.at[c, k],
+            device_id=(peer, vis),
+            device_id_type=pl.DeviceIdType.MESH,
+        )
+
+    def ring_arrival(c, k):
+        peer = lax.rem(tile + tiles - k, tiles)
+        return pltpu.make_async_remote_copy(
+            src_ref=sent_ref.at[c, peer],
+            dst_ref=landed.at[c, peer],
+            send_sem=ring_send.at[c, k],
+            recv_sem=ring_recv.at[c, k],
+            device_id=(peer, vis),
+            device_id_type=pl.DeviceIdType.MESH,
+        )
+
+    @pl.loop(0, chunks)
+    def _(c):
+        @pl.loop(1, tiles)
+        def _(k):
+            ring(c, k).start()
+
+    spots = lax.broadcasted_iota(jnp.int32, (own, slots), 0)
+    for q in range(quarters):
+        select[q * own : (q + 1) * own] = jnp.where(
+            spots + q * own == spot_ref[...], 1.0, 0.0
+        ).astype(BF16)
+    edge = jnp.zeros((chunks, RIM, chunk), F32)
+
+    @pl.when(jnp.logical_not(has_down))
+    def _():
+        sheet[:, 0:RIM] = edge
+
+    @pl.when(jnp.logical_not(has_up))
+    def _():
+        sheet[:, RIM + own : 2 * RIM + own] = edge
+
+    def hop(held, c, q, sends, recvs, step, source):
+        return pltpu.make_async_remote_copy(
+            src_ref=source.at[c, q],
+            dst_ref=held.at[c, q],
+            send_sem=sends.at[c, q],
+            recv_sem=recvs.at[c, q],
+            device_id=(tile, vis + step),
+            device_id_type=pl.DeviceIdType.MESH,
+        )
+
+    def forward(c, rightward):
+        held, sends, recvs, step = (
+            (right, right_send, right_recv, 1) if rightward else (left, left_send, left_recv, -1)
+        )
+        opens = first if rightward else last
+        order = reversed(range(quarters)) if rightward else range(quarters)
+        for q in order:
+            beyond = vis < q if rightward else vis > q
+
+            @pl.when(jnp.logical_and(beyond, opens))
+            def _():
+                hop(held, c, q, sends, recvs, step, part).start()
+
+            @pl.when(jnp.logical_and(beyond, jnp.logical_not(opens)))
+            def _():
+                hop(held, c, q, sends, recvs, step, held).wait_recv()
+                held[c, q] += part[c, q]
+                hop(held, c, q, sends, recvs, step, held).start()
+
+    def rim(c, upward):
+        src = sheet.at[c, pl.ds(own, RIM)] if upward else sheet.at[c, pl.ds(RIM, RIM)]
+        dst = sheet.at[c, pl.ds(0, RIM)] if upward else sheet.at[c, pl.ds(RIM + own, RIM)]
+        way = 0 if upward else 1
+        return pltpu.make_async_remote_copy(
+            src_ref=src,
+            dst_ref=dst,
+            send_sem=rim_send.at[c, way],
+            recv_sem=rim_recv.at[c, way],
+            device_id=up if upward else down,
+            device_id_type=pl.DeviceIdType.MESH,
+        )
+
+    @pl.loop(0, chunks + quarters - 1)
+    def _(turn):
+        @pl.when(turn < chunks)
+        def _():
+            c = turn
+
+            @pl.loop(1, tiles)
+            def _(k):
+                ring_arrival(c, k).wait_recv()
+
+            landed[c, tile] = sent_ref[c, tile]
+            top, rest = halves(landed[c].reshape(slots, chunk))
+
+            @pl.loop(0, quarters)
+            def _(q):
+                rows = select[pl.ds(pl.multiple_of(q * own, own), own), :]
+                part[c, q] = dot(rows, top) + dot(rows, rest)
+
+        for stage in range(quarters - 1):
+            c = turn - stage
+
+            @pl.when(jnp.logical_and(c >= 0, c < chunks))
+            def _():
+                @pl.when(vis == stage)
+                def _():
+                    forward(c, True)
+
+                @pl.when(vis == quarters - 1 - stage)
+                def _():
+                    forward(c, False)
+
+        c = turn - (quarters - 1)
+
+        @pl.when(c >= 0)
+        def _():
+            total = part[c, vis]
+            sheet[c, RIM : RIM + own] = total
+
+            @pl.when(vis > 0)
+            def _():
+                hop(right, c, vis, right_send, right_recv, 0, part).wait_recv()
+                sheet[c, RIM : RIM + own] += right[c, vis]
+
+            @pl.when(vis < quarters - 1)
+            def _():
+                hop(left, c, vis, left_send, left_recv, 0, part).wait_recv()
+                sheet[c, RIM : RIM + own] += left[c, vis]
+
+            sheet[c, RIM : RIM + own] *= inverse_ref[...]
+
+            @pl.when(has_up)
+            def _():
+                rim(c, True).start()
+
+            @pl.when(has_down)
+            def _():
+                rim(c, False).start()
+
+    for c in range(chunks):
+        coadd_ref[:, c * chunk : (c + 1) * chunk] = sheet[c, RIM : RIM + own]
+
+        @pl.when(has_down)
+        def _():
+            rim(c, True).wait_recv()
+
+        @pl.when(has_up)
+        def _():
+            rim(c, False).wait_recv()
+
+    b_top, b_rest = band_top_ref[...], band_rest_ref[...]
+    columns = []
+    for c in range(chunks):
+        s_top, s_rest = halves(sheet[c])
+        columns.append(dot(b_top, s_top) + (dot(b_rest, s_top) + dot(b_top, s_rest)))
+    top, rest = halves(windows_of(jnp.concatenate(columns, axis=1)))
+    swept = dot(top, top_ref[...]) + (dot(rest, top_ref[...]) + dot(top, rest_ref[...]))
+    for j in range(out_ref.shape[1] // LANES):
+        out_ref[:, j * LANES : (j + 1) * LANES] = swept[j * own : (j + 1) * own]
+
+    @pl.loop(0, chunks)
+    def _(c):
+        @pl.loop(1, tiles)
+        def _(k):
+            ring(c, k).wait_send()
+
+        @pl.when(has_up)
+        def _():
+            rim(c, True).wait_send()
+
+        @pl.when(has_down)
+        def _():
+            rim(c, False).wait_send()
+
+        for q in range(quarters):
+
+            @pl.when(vis < q)
+            def _():
+                hop(right, c, q, right_send, right_recv, 1, part).wait_send()
+
+            @pl.when(vis > q)
+            def _():
+                hop(left, c, q, left_send, left_recv, -1, part).wait_send()
+
+
+def combine(sent, spots, inverse, tiles, quarters):
+    chunks, _, span, chunk = sent.shape
+    width = chunks * chunk
+    own = SR // quarters
+    top, rest = halves_np(detect_taps(window_lags(), REACH))
+    lag = np.arange(own + 2 * RIM)[None, :] - RIM - np.arange(own)[:, None]
+    band_top, band_rest = halves_np(detect_taps(lag, REACH))
+    result = jax.ShapeDtypeStruct((own, width), F32)
+    held = pltpu.VMEM((chunks, quarters, own, chunk), F32)
+    pair = pltpu.SemaphoreType.DMA((chunks, tiles))
+    step = pltpu.SemaphoreType.DMA((chunks, quarters))
+    side = pltpu.SemaphoreType.DMA((chunks, 2))
     return pl.pallas_call(
-        gather_body,
-        grid_spec=pltpu.PrefetchScalarGridSpec(
-            num_scalar_prefetch=1,
-            grid=(1,),
-            in_specs=[pl.BlockSpec(landed.shape, lambda i, r: (0, 0, 0))],
-            out_specs=pl.BlockSpec((blocks, rows, width), lambda i, r: (0, 0, 0)),
+        functools.partial(combine_body, tiles, quarters),
+        out_shape=(result, result),
+        in_specs=[pl.BlockSpec(memory_space=pltpu.VMEM)] * 7,
+        out_specs=[pl.BlockSpec(memory_space=pltpu.VMEM)] * 2,
+        scratch_shapes=[
+            pltpu.VMEM(sent.shape, F32),
+            pltpu.VMEM((SR, tiles * span), BF16),
+            held,
+            held,
+            held,
+            pltpu.VMEM((chunks, own + 2 * RIM, chunk), F32),
+            pair, pair, step, step, step, step, side, side,
+        ],
+        compiler_params=pltpu.CompilerParams(
+            vmem_limit_bytes=52 * 2**20, collective_id=0, has_side_effects=True
         ),
-        out_shape=jax.ShapeDtypeStruct((blocks, rows, width), F32),
-        compiler_params=pltpu.CompilerParams(vmem_limit_bytes=50 * 2**20),
-        name="scatter_add",
-    )(spots, landed)
-
-
-def detect_body(above_ref, here_ref, below_ref, top_ref, rest_ref, band_top_ref, band_rest_ref, out_ref):
-    cells = jnp.concatenate([above_ref[...], here_ref[...], below_ref[...]], axis=0)
-    rows, width = cells.shape
-    top, rest = halves(windows_of(cells))
-    swept = dot(top, top_ref[...]) + (dot(rest, top_ref[...]) + dot(top, rest_ref[...]))
-    sheet = jnp.concatenate(
-        [swept[j * rows : (j + 1) * rows] for j in range(width // LANES)], axis=1
-    )
-    s_top, s_rest = halves(sheet)
-    b_top, b_rest = band_top_ref[...], band_rest_ref[...]
-    out_ref[...] = dot(b_top, s_top) + (dot(b_rest, s_top) + dot(b_top, s_rest))
-
-
-def detect(above, here, below):
-    rows = here.shape[0]
-    top, rest = halves_np(detect_taps(window_lags(), REACH))
-    lag = np.arange(rows + 2 * RIM)[None, :] - RIM - np.arange(rows)[:, None]
-    band_top, band_rest = halves_np(detect_taps(lag, REACH))
-    return pl.pallas_call(
-        detect_body,
-        out_shape=jax.ShapeDtypeStruct(here.shape, F32),
-        compiler_params=pltpu.CompilerParams(vmem_limit_bytes=50 * 2**20),
-        name="detect",
-    )(above, here, below, top, rest, band_top, band_rest)
+        name="combine",
+    )(spots, inverse, sent, top, rest, band_top, band_rest)
 
 
 def shards(pieces, coeffs, weights, routes, offsets):
@@ -214,9 +432,7 @@
     facts = jnp.stack([target.astype(F32), offsets.astype(F32), weights])
     known = lax.all_gather(facts, ("tile", "vis"))
     sent = match(pieces, mix_table(coeffs, weights, rows), target, tiles, capacity)
-    sent = sent.reshape(tiles, capacity, rows, width)
-    landed = lax.all_to_all(sent, "tile", split_axis=0, concat_axis=0, tiled=True)
-    landed = landed.reshape(tiles * capacity, rows, width)
+    sent = sent.reshape(width // CHUNK, tiles, capacity * rows, CHUNK)
     mine = known[:, 0] == me_tile.astype(F32)
     grid_of = jnp.arange(blocks).astype(F32)
     near_vis = lax.dynamic_slice_in_dim(
@@ -227,22 +443,14 @@
     rank = jnp.sum(jnp.where(earlier[None] & hit[:, None, :], 1, 0), axis=2)
     slot_hit = hit[:, None, :] & (rank[:, None, :] == jnp.arange(capacity)[None, :, None])
     spots = jnp.sum(jnp.where(slot_hit, near_vis[:, None, 1], 0.0), axis=2)
-    spots = spots.astype(jnp.int32).reshape(-1)
+    spots = spots.astype(jnp.int32).reshape(-1, 1) * rows + jnp.arange(rows)
     own_blocks = blocks // quarters
     own_grid = (me_vis * own_blocks + jnp.arange(own_blocks)).astype(F32)
     on_block = mine[None] & (known[:, 1][None] == own_grid[:, None, None])
     masses = jnp.sum(jnp.where(on_block, known[:, 2][None], 0.0), axis=(1, 2))
     inverse = jnp.where(masses > 0.0, 1.0 / jnp.where(masses > 0.0, masses, 1.0), 0.0)
-    numerator = scatter_add(landed, spots, blocks)
-    summed = lax.psum_scatter(numerator, "vis", scatter_dimension=0, tiled=True)
-    coadd = jnp.where(
-        (masses > 0.0)[:, None, None], summed * inverse[:, None, None], 0.0
-    ).reshape(own_blocks * rows, width)
-    total = tiles * quarters
-    both = ("tile", "vis")
-    above = lax.ppermute(coadd[-RIM:], both, [(i, i + 1) for i in range(total - 1)])
-    below = lax.ppermute(coadd[:RIM], both, [(i + 1, i) for i in range(total - 1)])
-    return coadd, detect(above, coadd, below)
+    inverse = jnp.broadcast_to(inverse[:, None, None], (own_blocks, rows, CHUNK))
+    return combine(sent, spots.reshape(1, -1), inverse.reshape(-1, CHUNK), tiles, quarters)
 
 
 def solution(mesh):

time: 211 us -> 201 us (0.953); the launches traced: 211 us -> 198 us
  Pallas kernels: 19.3 us -> 109 us
  waiting for transfers between devices: 81 us -> 0 us
  between operations: 14.3 us -> 0.8 us
  starting transfers between devices: 11.7 us -> 0 us
  local copies, waits for them, and re-layouts: 10.8 us -> 14.4 us
    pallas_call x2 -> x1, Pallas kernels: 9.88 us -> 99.9 us  [combine(): pl.pallas_call(functools.partial(combine_body, tiles, quarters), out_shap...]
    reduce_scatter x1 -> x0, waiting for transfers between devices: 73.8 us -> none  [shards(): summed = lax.psum_scatter(numerator, 'vis', scatter_dimension=0, tiled=True)]
    ppermute x2 -> x0, waiting for transfers between devices: 7.24 us -> none  [the longest x1 7.24 us: shards(): lax.ppermute(coadd[-RIM:], both, [(i, i + 1) for i in range(total - 1)])]
    ppermute x2 -> x0, starting transfers between devices: 7.05 us -> none  [the longest x1 5.13 us: shards(): lax.ppermute(coadd[:RIM], both, [(i + 1, i) for i in range(total - 1)])]
    all_to_all x1 -> x0, starting transfers between devices: 4.64 us -> none  [shards(): lax.all_to_all(sent, 'tile', split_axis=0, concat_axis=0, tiled=True)]
    unnamed x25 -> x19, local copies, waits for them, and re-layouts: 0.05 us -> 3.33 us
  transfers between devices with their start and end apart: 4 -> 0, of which waited for: 2 -> 0; matrix products, arithmetic and copies ran while one was open for 0% -> 0% of each run, Pallas kernels for 0% -> 0%
where the time goes in v2:
time: 201 us; the launch traced here: 198 us
  Pallas kernels  109 us (54%)
  blocking collectives  67.7 us (34%)
  local copies, waits for them, and re-layouts  14.4 us (7%)
  other arithmetic  4.14 us (2%)
    pallas_call x1, Pallas kernels, combine(): pl.pallas_call(functools.partial(combine_body, tiles, quarters), out_shap...  99.9 us
    all_gather x1, blocking collectives, shards(): known = lax.all_gather(facts, ('tile', 'vis'))  67.7 us
    broadcast_in_dim x5, local copies, waits for them, and re-layouts, mix_table(): jnp.where(same, each, 0.0)  9.66 us
    pallas_call x1, Pallas kernels, match(): pl.pallas_call(functools.partial(match_body, capacity), grid_spec=pltpu.P...  9.36 us

profile of v2, /device:TPU:4, one launch (start us, length us, event | category | flops | bytes accessed | tf_op | source)
XLA Modules:
  0.0 197.8 jit_solution(3707783514059373225)
XLA Ops:
  0.6 0.7 convert_bitcast_fusion
  1.3 0.7 convert_bitcast_fusion.1
  2.0 0.7 maximum_bitcast_fusion
  2.6 0.7 multiply_bitcast_fusion
  3.3 67.7 %all-gather.1 = f32[32,3,32]{2,1,0:T(4,128)S(1)} all-gather(f32[1,3,32]{2,1,0:T(4,128)S(1)} %maximum_bitcast_fusion), channel_id=2, replica_groups=mesh['tile'=8,'vis'=4] {'tile','vis'}, dimensions={0}, use_global_device_ids=true | all-gather | bytes 12672 | tf_op jit(solution)/shard_map/all_gather | solution.py:433
  71.0 0.9 select_reduce_fusion.1
  72.0 0.1 select_reduce_fusion.2
  72.1 0.1 mul.27
  72.1 0.1 iota_add_fusion
  72.2 0.1 add.40.spot_ref
  72.4 0.3 select_reduce_fusion
  72.7 0.1 broadcast_in_dim.95
  72.7 0.1 broadcast_in_dim.96
  72.8 0.8 broadcast_in_dim.99
  73.6 0.3 broadcast_in_dim.100
  73.9 0.1 broadcast_in_dim.97.inverse_ref
  74.0 1.5 convolution_bitcast_fusion
  75.5 1.0 copy.30
  76.5 0.4 copy.31
  76.9 2.7 %broadcast_in_dim.103 = f32[8,4,16,4,4,16]{5,4,3,2,1,0:T(4,128)} broadcast(f32[8,4,16,4,16]{4,3,2,1,0:T(4,128)S(1)} %copy.31), dimensions={0,1,2,3,5} | broadcast | bytes 655360 | tf_op jit(solution)/shard_map/jit(_where)/broadcast_in_dim | solution.py:157
  79.7 0.0 copy-start
  79.7 0.0 copy-start.1
  79.7 0.0 copy-start.2
  79.7 0.0 copy-start.7
  79.7 5.4 %broadcast_in_dim.104 = f32[8,64,256]{2,1,0:T(8,128)S(1)} reshape(f32[8,4,16,4,4,16]{5,4,3,2,1,0:T(4,128)} %broadcast_in_dim.103) | data formatting | bytes 1048576 | tf_op jit(solution)/shard_map/jit(_where)/broadcast_in_dim | solution.py:157
  85.1 0.0 copy-start.3
  85.1 0.0 copy-start.4
  85.1 0.0 copy-start.5
  85.1 0.0 copy-start.6
  85.2 0.0 copy-done
  85.2 0.0 copy-done.1
  85.2 0.0 copy-done.2
  85.2 0.0 copy-done.7
  85.2 9.4 %match.1 = f32[4,64,16,256]{3,2,1,0:T(8,128)} custom-call(s32[32]{0:T(128)S(1)} %bitcast.30, f32[32,16,1024]{2,1,0:T(8,128)S(1)} %copy-done, f32[8,64,256]{2,1,0:T(8,128)S(1)} %broadcast_select_fusion.mix_ref, bf16[256,512]{1,0:T(8,128)(2,1)S(1)} %copy-done.2, bf16[256,512]{1,0:T(8,128)(2,1)S(1)} %copy-done.1), custom_call_target="tpu_custom_call" | custom-call | tf_op jit(solution)/shard_map/match/pallas_call | solution.py:129
  94.6 0.0 copy-done.3
  94.6 0.0 copy-done.4
  94.6 0.0 copy-done.5
  94.6 0.0 copy-done.6
  94.6 99.9 %combine.1 = (f32[256,1024]{1,0:T(8,128)S(1)}, f32[256,1024]{1,0:T(8,128)}) custom-call(s32[1,1024]{1,0:T(1,128)S(1)} %add.40.spot_ref, f32[256,256]{1,0:T(8,128)S(1)} %broadcast_in_dim.97.inverse_ref, f32[4,8,128,256]{3,2,1,0:T(8,128)} %bitcast.31, bf16[256,128]{1,0:T(8,128)(2,1)S(1)} %copy-done.6, bf16[256,128]{1,0:T(8,128)(2,1)S(1)} %copy-done.5, ...), custom_call_target="tpu_custom_call" | custom-call | tf_op jit(solution)/shard_map/combine/pallas_call | solution.py:404
  194.5 1.0 copy.43
  195.5 2.3 %copy.44 = f32[256,1024]{1,0:T(8,128)} copy(f32[256,1024]{1,0:T(8,128)} %get-tuple-element.8) | data formatting | bytes 2097152
  (10 shorter events, 0.1 us)
Async XLA Ops:
  79.7 5.6 %copy-start = (f32[32,16,1024]{2,1,0:T(8,128)S(1)}, f32[32,16,1024]{2,1,0:T(8,128)}, u32[]{:S(2)}) copy-start(f32[32,16,1024]{2,1,0:T(8,128)} %pieces_ref.1) | copy-start | bytes 6291460
  79.7 5.6 %copy-start.1 = (bf16[256,512]{1,0:T(8,128)(2,1)S(1)}, bf16[256,512]{1,0:T(8,128)(2,1)}, u32[]{:S(2)}) copy-start(bf16[256,512]{1,0:T(8,128)(2,1)} %constant.45.clone.rest_ref) | copy-start | bytes 786436
  79.7 5.6 %copy-start.2 = (bf16[256,512]{1,0:T(8,128)(2,1)S(1)}, bf16[256,512]{1,0:T(8,128)(2,1)}, u32[]{:S(2)}) copy-start(bf16[256,512]{1,0:T(8,128)(2,1)} %constant.44.clone.top_ref) | copy-start | bytes 786436
  79.7 5.6 %copy-start.7 = (s32[32,1]{0,1:T(1,128)S(1)}, s32[32,1]{0,1:T(1,128)}, u32[]{:S(2)}) copy-start(s32[32,1]{0,1:T(1,128)} %param.17) | copy-start | bytes 388
  85.1 9.5 %copy-start.3 = (bf16[256,288]{1,0:T(8,128)(2,1)S(1)}, bf16[256,288]{1,0:T(8,128)(2,1)}, u32[]{:S(2)}) copy-start(bf16[256,288]{1,0:T(8,128)(2,1)} %constant.50.clone.band_rest_ref) | copy-start | bytes 442372
  85.1 9.5 %copy-start.4 = (bf16[256,288]{1,0:T(8,128)(2,1)S(1)}, bf16[256,288]{1,0:T(8,128)(2,1)}, u32[]{:S(2)}) copy-start(bf16[256,288]{1,0:T(8,128)(2,1)} %constant.49.clone.band_top_ref) | copy-start | bytes 442372
  85.1 9.5 %copy-start.5 = (bf16[256,128]{1,0:T(8,128)(2,1)S(1)}, bf16[256,128]{1,0:T(8,128)(2,1)}, u32[]{:S(2)}) copy-start(bf16[256,128]{1,0:T(8,128)(2,1)} %constant.48.clone.rest_ref) | copy-start | bytes 196612
  85.1 9.5 %copy-start.6 = (bf16[256,128]{1,0:T(8,128)(2,1)S(1)}, bf16[256,128]{1,0:T(8,128)(2,1)}, u32[]{:S(2)}) copy-start(bf16[256,128]{1,0:T(8,128)(2,1)} %constant.47.clone.top_ref) | copy-start | bytes 196612

commit v3 on v2

--- a/solution.py
+++ b/solution.py
@@ -20,7 +20,6 @@
 
 row_shapes = ((1.0, 0), (1.0, 1), (2.0, 0), (2.0, 2), (3.5, 0))
 column_shapes = ((1.0, 0), (2.0, 0), (2.0, 1), (3.5, 0))
-highest = lax.Precision.HIGHEST
 F32 = jnp.float32
 BF16 = jnp.bfloat16
 
@@ -75,7 +74,10 @@
     )
 
 
-def match_body(capacity, routes_ref, pieces_ref, mix_ref, top_ref, rest_ref, out_ref, count_ref):
+def match_body(
+    capacity, routes_ref, offsets_ref, weights_ref, coeffs_ref,
+    pieces_ref, bank_ref, top_ref, rest_ref, out_ref, note_ref, count_ref,
+):
     step = pl.program_id(0)
     pieces, rows, width = pieces_ref.shape
     kinds = top_ref.shape[1] // LANES
@@ -84,6 +86,7 @@
     @pl.when(step == 0)
     def _():
         out_ref[...] = jnp.zeros_like(out_ref)
+        note_ref[...] = jnp.full_like(note_ref, -1.0)
 
         @pl.loop(0, count_ref.shape[0])
         def _(i):
@@ -94,6 +97,23 @@
     top, rest = halves(wide)
     swept = dot(top, top_ref[...]) + (dot(rest, top_ref[...]) + dot(top, rest_ref[...]))
     span = GROUP * rows
+    kinds_row, _, depth = bank_ref.shape
+    lane = lax.broadcasted_iota(jnp.int32, (1, depth), 1)
+    note_lane = lax.broadcasted_iota(jnp.int32, note_ref.shape[1:], 1)
+    note_row = lax.broadcasted_iota(jnp.int32, note_ref.shape[1:], 0)
+
+    def mix_of(piece, place):
+        total = None
+        for a in range(kinds_row):
+            base = (piece * kinds_row + a) * kinds
+            row = jnp.full((1, depth), coeffs_ref[base], F32)
+            for b in range(1, kinds):
+                row = jnp.where(lane >= b * span, coeffs_ref[base + b], row)
+            term = row * bank_ref[a]
+            total = term if total is None else total + term
+        keep = jnp.logical_and(lane % span >= place * rows, lane % span < (place + 1) * rows)
+        return jnp.where(keep, total * weights_ref[piece], 0.0)
+
     for q in range(pieces // GROUP):
         parts = []
         for j in range(blocks):
@@ -106,64 +126,68 @@
             )
         banked = jnp.concatenate(parts, axis=1)
         y_top, y_rest = halves(banked)
-        m_top, m_rest = halves(mix_ref[q])
+        lead = step * pieces + q * GROUP
+        m_top, m_rest = halves(
+            jnp.concatenate([mix_of(lead + i, i) for i in range(GROUP)], axis=0)
+        )
         result = dot(m_top, y_top) + (dot(m_rest, y_top) + dot(m_top, y_rest))
         for i in range(GROUP):
-            strip = routes_ref[step * pieces + q * GROUP + i]
+            piece = lead + i
+            strip = routes_ref[piece]
             rank = count_ref[strip]
             count_ref[strip] = rank + 1
+            fact = jnp.where(
+                note_row == 0,
+                (offsets_ref[piece] * rows + note_lane % rows).astype(F32),
+                weights_ref[piece],
+            )
+            here = jnp.logical_and(note_lane >= rank * rows, note_lane < (rank + 1) * rows)
+            note_ref[strip] = jnp.where(here, fact, note_ref[strip])
             for c in range(out_ref.shape[0]):
                 out_ref[c, strip * capacity + rank] = result[
                     i * rows : (i + 1) * rows, c * CHUNK : (c + 1) * CHUNK
                 ]
 
 
-def match(pieces, mix, routes, tiles, capacity):
+def match(pieces, coeffs, weights, routes, offsets, tiles, capacity):
     count, rows, width = pieces.shape
     batch = 8
+    kinds = coeffs.shape[2]
     top, rest = halves_np(
         np.concatenate(list(shaped_taps(window_lags(), column_shapes, TAPS)), axis=1)
     )
-    groups = batch // GROUP
+    lag = np.arange(rows)[None, :] - np.arange(rows)[:, None]
+    bank = np.tile(shaped_taps(lag, row_shapes, TAPS), (1, 1, kinds * GROUP)).astype(np.float32)
     shape = (width // CHUNK, tiles * capacity, rows, CHUNK)
+    note = (tiles, 8, -(-capacity * rows // LANES) * LANES)
     return pl.pallas_call(
         functools.partial(match_body, capacity),
         grid_spec=pltpu.PrefetchScalarGridSpec(
-            num_scalar_prefetch=1,
+            num_scalar_prefetch=4,
             grid=(count // batch,),
             in_specs=[
-                pl.BlockSpec((batch, rows, width), lambda i, r: (i, 0, 0)),
-                pl.BlockSpec((groups,) + mix.shape[1:], lambda i, r: (i, 0, 0)),
-                pl.BlockSpec(top.shape, lambda i, r: (0, 0)),
-                pl.BlockSpec(rest.shape, lambda i, r: (0, 0)),
+                pl.BlockSpec((batch, rows, width), lambda i, *r: (i, 0, 0)),
+                pl.BlockSpec(bank.shape, lambda i, *r: (0, 0, 0)),
+                pl.BlockSpec(top.shape, lambda i, *r: (0, 0)),
+                pl.BlockSpec(rest.shape, lambda i, *r: (0, 0)),
             ],
-            out_specs=pl.BlockSpec(shape, lambda i, r: (0, 0, 0, 0)),
+            out_specs=[
+                pl.BlockSpec(shape, lambda i, *r: (0, 0, 0, 0)),
+                pl.BlockSpec(note, lambda i, *r: (0, 0, 0)),
+            ],
             scratch_shapes=[pltpu.SMEM((tiles,), jnp.int32)],
         ),
-        out_shape=jax.ShapeDtypeStruct(shape, F32),
+        out_shape=(jax.ShapeDtypeStruct(shape, F32), jax.ShapeDtypeStruct(note, F32)),
         compiler_params=pltpu.CompilerParams(vmem_limit_bytes=50 * 2**20),
         name="match",
-    )(routes, pieces, mix, top, rest)
-
-
-def mix_table(coeffs, weights, rows):
-    count, kinds_row, kinds = coeffs.shape
-    lag = np.arange(rows)[None, :] - np.arange(rows)[:, None]
-    bank = jnp.asarray(shaped_taps(lag, row_shapes, TAPS).astype(np.float32))
-    weighted = coeffs * weights[:, None, None]
-    each = jnp.einsum("mab,aqp->mqbp", weighted, bank, precision=highest)
-    each = each.reshape(count // GROUP, GROUP, rows, kinds, 1, rows)
-    same = np.eye(GROUP, dtype=bool)[None, :, None, None, :, None]
-    return jnp.where(same, each, 0.0).reshape(
-        count // GROUP, GROUP * rows, kinds * GROUP * rows
-    )
+    )(routes, offsets, weights, coeffs.reshape(-1), pieces, jnp.asarray(bank), top, rest)
 
 
 def combine_body(
-    tiles, quarters, spot_ref, inverse_ref, sent_ref, top_ref, rest_ref, band_top_ref, band_rest_ref,
+    tiles, quarters, note_ref, sent_ref, top_ref, rest_ref, band_top_ref, band_rest_ref,
     coadd_ref, out_ref,
-    landed, select, part, right, left, sheet,
-    ring_send, ring_recv, right_send, right_recv, left_send, left_recv, rim_send, rim_recv,
+    landed, notes, select, part, right, left, sheet, inverse,
+    note_send, note_recv, ring_send, ring_recv, right_send, right_recv, left_send, left_recv, rim_send, rim_recv,
 ):
     tile, vis = lax.axis_index("tile"), lax.axis_index("vis")
     chunks, _, span, chunk = landed.shape
@@ -184,21 +208,41 @@
     def greet(device):
         pl.semaphore_signal(barrier, inc=1, device_id=device, device_id_type=pl.DeviceIdType.MESH)
 
-    @pl.loop(1, tiles)
+    everyone = tiles * quarters
+    me = tile * quarters + vis
+
+    @pl.loop(1, everyone)
     def _(k):
-        greet((lax.rem(tile + k, tiles), vis))
-
-    @pl.when(has_down)
-    def _():
-        greet(down)
-
-    @pl.when(has_up)
-    def _():
-        greet(up)
-
-    pl.semaphore_wait(
-        barrier, tiles - 1 + has_down.astype(jnp.int32) + has_up.astype(jnp.int32)
-    )
+        peer = lax.rem(me + k, everyone)
+        greet((lax.div(peer, quarters), lax.rem(peer, quarters)))
+
+    pl.semaphore_wait(barrier, everyone - 1)
+
+    def tell(k):
+        peer = lax.rem(me + k, everyone)
+        return pltpu.make_async_remote_copy(
+            src_ref=note_ref.at[lax.div(peer, quarters)],
+            dst_ref=notes.at[vis, tile],
+            send_sem=note_send.at[k],
+            recv_sem=note_recv.at[k],
+            device_id=(lax.div(peer, quarters), lax.rem(peer, quarters)),
+            device_id_type=pl.DeviceIdType.MESH,
+        )
+
+    def told(k):
+        peer = lax.rem(me + everyone - k, everyone)
+        return pltpu.make_async_remote_copy(
+            src_ref=note_ref.at[lax.div(peer, quarters)],
+            dst_ref=notes.at[lax.rem(peer, quarters), lax.div(peer, quarters)],
+            send_sem=note_send.at[k],
+            recv_sem=note_recv.at[k],
+            device_id=(lax.div(peer, quarters), lax.rem(peer, quarters)),
+            device_id_type=pl.DeviceIdType.MESH,
+        )
+
+    @pl.loop(1, everyone)
+    def _(k):
+        tell(k).start()
 
     def ring(c, k):
         peer = lax.rem(tile + k, tiles)
@@ -228,11 +272,28 @@
         def _(k):
             ring(c, k).start()
 
-    spots = lax.broadcasted_iota(jnp.int32, (own, slots), 0)
+    notes[vis, tile] = note_ref[tile]
+
+    @pl.loop(1, everyone)
+    def _(k):
+        told(k).wait_recv()
+
+    grid_rows = lax.broadcasted_iota(jnp.int32, (own, slots), 0).astype(F32)
+    spots = jnp.concatenate([notes[vis, t, 0:1, 0:span] for t in range(tiles)], axis=1)
     for q in range(quarters):
-        select[q * own : (q + 1) * own] = jnp.where(
-            spots + q * own == spot_ref[...], 1.0, 0.0
-        ).astype(BF16)
+        select[q * own : (q + 1) * own] = jnp.where(grid_rows + q * own == spots, 1.0, 0.0).astype(BF16)
+    own_rows = lax.broadcasted_iota(jnp.int32, (own, span), 0) + vis * own
+    own_rows = own_rows.astype(F32)
+
+    def weigh(i, total):
+        v, t = lax.rem(i, quarters), lax.div(i, quarters)
+        hit = own_rows == notes[v, t, 0:1, 0:span]
+        return total + jnp.where(hit, notes[v, t, 1:2, 0:span], 0.0)
+
+    masses = lax.fori_loop(0, everyone, weigh, jnp.zeros((own, span), F32))
+    mass = jnp.sum(masses, axis=1, keepdims=True)
+    scale = jnp.where(mass > 0.0, 1.0 / jnp.where(mass > 0.0, mass, 1.0), 0.0)
+    inverse[...] = jnp.broadcast_to(scale, (own, LANES))
     edge = jnp.zeros((chunks, RIM, chunk), F32)
 
     @pl.when(jnp.logical_not(has_down))
@@ -333,7 +394,8 @@
                 hop(left, c, vis, left_send, left_recv, 0, part).wait_recv()
                 sheet[c, RIM : RIM + own] += left[c, vis]
 
-            sheet[c, RIM : RIM + own] *= inverse_ref[...]
+            for j in range(chunk // LANES):
+                sheet[c, RIM : RIM + own, j * LANES : (j + 1) * LANES] *= inverse[...]
 
             @pl.when(has_up)
             def _():
@@ -364,6 +426,10 @@
     for j in range(out_ref.shape[1] // LANES):
         out_ref[:, j * LANES : (j + 1) * LANES] = swept[j * own : (j + 1) * own]
 
+    @pl.loop(1, everyone)
+    def _(k):
+        tell(k).wait_send()
+
     @pl.loop(0, chunks)
     def _(c):
         @pl.loop(1, tiles)
@@ -389,7 +455,7 @@
                 hop(left, c, q, left_send, left_recv, -1, part).wait_send()
 
 
-def combine(sent, spots, inverse, tiles, quarters):
+def combine(sent, note, tiles, quarters):
     chunks, _, span, chunk = sent.shape
     width = chunks * chunk
     own = SR // quarters
@@ -398,59 +464,40 @@
     band_top, band_rest = halves_np(detect_taps(lag, REACH))
     result = jax.ShapeDtypeStruct((own, width), F32)
     held = pltpu.VMEM((chunks, quarters, own, chunk), F32)
+    every = pltpu.SemaphoreType.DMA((tiles * quarters,))
     pair = pltpu.SemaphoreType.DMA((chunks, tiles))
     step = pltpu.SemaphoreType.DMA((chunks, quarters))
     side = pltpu.SemaphoreType.DMA((chunks, 2))
     return pl.pallas_call(
         functools.partial(combine_body, tiles, quarters),
         out_shape=(result, result),
-        in_specs=[pl.BlockSpec(memory_space=pltpu.VMEM)] * 7,
+        in_specs=[pl.BlockSpec(memory_space=pltpu.VMEM)] * 6,
         out_specs=[pl.BlockSpec(memory_space=pltpu.VMEM)] * 2,
         scratch_shapes=[
             pltpu.VMEM(sent.shape, F32),
+            pltpu.VMEM((quarters,) + note.shape, F32),
             pltpu.VMEM((SR, tiles * span), BF16),
             held,
             held,
             held,
             pltpu.VMEM((chunks, own + 2 * RIM, chunk), F32),
-            pair, pair, step, step, step, step, side, side,
+            pltpu.VMEM((own, LANES), F32),
+            every, every, pair, pair, step, step, step, step, side, side,
         ],
         compiler_params=pltpu.CompilerParams(
             vmem_limit_bytes=52 * 2**20, collective_id=0, has_side_effects=True
         ),
         name="combine",
-    )(spots, inverse, sent, top, rest, band_top, band_rest)
+    )(note, sent, top, rest, band_top, band_rest)
 
 
 def shards(pieces, coeffs, weights, routes, offsets):
     tiles, quarters = lax.axis_size("tile"), lax.axis_size("vis")
-    me_tile, me_vis = lax.axis_index("tile"), lax.axis_index("vis")
     count, rows, width = pieces.shape
     capacity = max(2, 2 * count // tiles)
-    blocks = SR // rows
-    target = routes[:, 0]
-    facts = jnp.stack([target.astype(F32), offsets.astype(F32), weights])
-    known = lax.all_gather(facts, ("tile", "vis"))
-    sent = match(pieces, mix_table(coeffs, weights, rows), target, tiles, capacity)
+    sent, note = match(pieces, coeffs, weights, routes[:, 0], offsets, tiles, capacity)
     sent = sent.reshape(width // CHUNK, tiles, capacity * rows, CHUNK)
-    mine = known[:, 0] == me_tile.astype(F32)
-    grid_of = jnp.arange(blocks).astype(F32)
-    near_vis = lax.dynamic_slice_in_dim(
-        known.reshape(tiles, quarters, 3, count), me_vis, 1, 1
-    )[:, 0]
-    hit = near_vis[:, 0] == me_tile.astype(F32)
-    earlier = np.arange(count)[None, :] < np.arange(count)[:, None]
-    rank = jnp.sum(jnp.where(earlier[None] & hit[:, None, :], 1, 0), axis=2)
-    slot_hit = hit[:, None, :] & (rank[:, None, :] == jnp.arange(capacity)[None, :, None])
-    spots = jnp.sum(jnp.where(slot_hit, near_vis[:, None, 1], 0.0), axis=2)
-    spots = spots.astype(jnp.int32).reshape(-1, 1) * rows + jnp.arange(rows)
-    own_blocks = blocks // quarters
-    own_grid = (me_vis * own_blocks + jnp.arange(own_blocks)).astype(F32)
-    on_block = mine[None] & (known[:, 1][None] == own_grid[:, None, None])
-    masses = jnp.sum(jnp.where(on_block, known[:, 2][None], 0.0), axis=(1, 2))
-    inverse = jnp.where(masses > 0.0, 1.0 / jnp.where(masses > 0.0, masses, 1.0), 0.0)
-    inverse = jnp.broadcast_to(inverse[:, None, None], (own_blocks, rows, CHUNK))
-    return combine(sent, spots.reshape(1, -1), inverse.reshape(-1, CHUNK), tiles, quarters)
+    return combine(sent, note, tiles, quarters)
 
 
 def solution(mesh):

time: 201 us -> 131 us (0.65); the launches traced: 198 us -> 131 us
  blocking collectives: 67.7 us -> 0 us
  Pallas kernels: 109 us -> 116 us
  other arithmetic: 4.14 us -> 0 us
    all_gather x1 -> x0, blocking collectives: 67.7 us -> none  [shards(): known = lax.all_gather(facts, ('tile', 'vis'))]
    unnamed x19 -> x25, local copies, waits for them, and re-layouts: 3.33 us -> 14 us
    broadcast_in_dim x9 -> x0, local copies, waits for them, and re-layouts: 9.91 us -> none  [the longest x5 9.66 us: mix_table(): jnp.where(same, each, 0.0)]
    pallas_call x1, Pallas kernels: 99.9 us -> 107 us  [combine(): pl.pallas_call(functools.partial(combine_body, tiles, quarters), out_shap...]
where the time goes in v3:
time: 131 us
  Pallas kernels  116 us (89%)
  local copies, waits for them, and re-layouts  14.1 us (11%)
    pallas_call x1, Pallas kernels, combine(): pl.pallas_call(functools.partial(combine_body, tiles, quarters), out_shap...  107 us
    unnamed x25, local copies, waits for them, and re-layouts  14 us
    pallas_call x1, Pallas kernels, match(): pl.pallas_call(functools.partial(match_body, capacity), grid_spec=pltpu.P...  9.1 us

profile of v3, /device:TPU:4, one launch (start us, length us, event | category | flops | bytes accessed | tf_op | source)
XLA Modules:
  0.0 130.9 jit_solution(17024877640591445417)
XLA Ops:
  0.6 0.8 copy.14
  1.5 0.1 reshape.10.coeffs_ref
  1.6 0.0 copy-start
  1.6 1.6 %copy-done = f32[32,16,1024]{2,1,0:T(8,128)S(1)} copy-done((f32[32,16,1024]{2,1,0:T(8,128)S(1)}, f32[32,16,1024]{2,1,0:T(8,128)}, u32[]{:S(2)}) %copy-start) | copy-done | bytes 2097176
  3.2 0.0 copy-start.1
  3.2 0.9 copy-done.1
  4.1 0.0 copy-start.2
  4.1 0.9 copy-done.2
  5.1 0.0 copy-start.5
  5.1 0.9 copy-done.5
  6.0 0.0 copy-start.8
  6.0 0.7 copy-done.8
  6.6 0.0 copy-start.9
  6.6 0.7 copy-done.9
  7.3 0.0 copy-start.10
  7.3 0.7 copy-done.10
  7.9 9.1 %match.1 = (f32[4,64,16,256]{3,2,1,0:T(8,128)}, f32[8,8,128]{2,1,0:T(8,128)S(1)}) custom-call(s32[32]{0:T(128)S(1)} %bitcast.2, s32[32]{0:T(128)S(1)} %copy-done.9, f32[32]{0:T(128)S(1)} %copy-done.10, f32[640]{0:T(1024)S(1)} %reshape.10.coeffs_ref, f32[32,16,1024]{2,1,0:T(8,128)S(1)} %copy-done, f32[5,16,256]{2,1,0:T(8,128)S(1)} %copy-done.5, ...), custom_call_target="tpu_custom_call" | custom-call | tf_op jit(solution)/shard_map/match/pallas_call | solution.py:163
  17.0 0.0 copy-start.3
  17.0 0.9 copy-done.3
  17.9 0.0 copy-start.4
  17.9 0.9 copy-done.4
  18.9 0.0 copy-start.6
  18.9 0.8 copy-done.6
  19.7 0.0 copy-start.7
  19.7 0.8 copy-done.7
  20.5 107.0 %combine.1 = (f32[256,1024]{1,0:T(8,128)S(1)}, f32[256,1024]{1,0:T(8,128)}) custom-call(f32[8,8,128]{2,1,0:T(8,128)S(1)} %get-tuple-element.4.note_ref, f32[4,8,128,256]{3,2,1,0:T(8,128)} %bitcast.3, bf16[256,128]{1,0:T(8,128)(2,1)S(1)} %copy-done.7, bf16[256,128]{1,0:T(8,128)(2,1)S(1)} %copy-done.6, bf16[256,288]{1,0:T(8,128)(2,1)S(1)} %copy-done.4, ...), custom_call_target="tpu_custom_call" | custom-call | tf_op jit(solution)/shard_map/combine/pallas_call | solution.py:471
  127.6 1.0 copy.17
  128.6 2.3 %copy.18 = f32[256,1024]{1,0:T(8,128)} copy(f32[256,1024]{1,0:T(8,128)} %get-tuple-element.9) | data formatting | bytes 2097152
Async XLA Ops:
  1.6 1.6 %copy-start = (f32[32,16,1024]{2,1,0:T(8,128)S(1)}, f32[32,16,1024]{2,1,0:T(8,128)}, u32[]{:S(2)}) copy-start(f32[32,16,1024]{2,1,0:T(8,128)} %pieces_ref.1) | copy-start | bytes 6291460
  3.2 0.9 copy-start.1
  4.1 0.9 copy-start.2
  5.1 0.9 copy-start.5
  6.0 0.7 copy-start.8
  6.6 0.7 copy-start.9
  7.3 0.7 copy-start.10
  17.0 0.9 copy-start.3
  17.9 0.9 copy-start.4
  18.9 0.8 copy-start.6
  19.7 0.8 copy-start.7

commit v4 on v3

--- a/solution.py
+++ b/solution.py
@@ -16,7 +16,7 @@
 SIDE = 64
 RIM = 16
 GROUP = 4
-CHUNK = 256
+CHUNK = 128
 
 row_shapes = ((1.0, 0), (1.0, 1), (2.0, 0), (2.0, 2), (3.5, 0))
 column_shapes = ((1.0, 0), (2.0, 0), (2.0, 1), (3.5, 0))
@@ -48,7 +48,7 @@
     table = table.astype(np.float32)
     top = table.astype(ml_dtypes.bfloat16)
     rest = (table - top.astype(np.float32)).astype(ml_dtypes.bfloat16)
-    return jnp.asarray(top), jnp.asarray(rest)
+    return jnp.asarray(np.stack([top, rest]))
 
 
 def halves(x):
@@ -76,11 +76,11 @@
 
 def match_body(
     capacity, routes_ref, offsets_ref, weights_ref, coeffs_ref,
-    pieces_ref, bank_ref, top_ref, rest_ref, out_ref, note_ref, count_ref,
+    pieces_ref, bank_ref, taps_ref, out_ref, note_ref, count_ref,
 ):
     step = pl.program_id(0)
     pieces, rows, width = pieces_ref.shape
-    kinds = top_ref.shape[1] // LANES
+    kinds = taps_ref.shape[2] // LANES
     blocks = width // LANES
 
     @pl.when(step == 0)
@@ -95,7 +95,7 @@
     flat = pieces_ref[...].reshape(pieces * rows, width)
     wide = windows_of(flat)
     top, rest = halves(wide)
-    swept = dot(top, top_ref[...]) + (dot(rest, top_ref[...]) + dot(top, rest_ref[...]))
+    swept = dot(top, taps_ref[0]) + (dot(rest, taps_ref[0]) + dot(top, taps_ref[1]))
     span = GROUP * rows
     kinds_row, _, depth = bank_ref.shape
     lane = lax.broadcasted_iota(jnp.int32, (1, depth), 1)
@@ -153,7 +153,7 @@
     count, rows, width = pieces.shape
     batch = 8
     kinds = coeffs.shape[2]
-    top, rest = halves_np(
+    taps = halves_np(
         np.concatenate(list(shaped_taps(window_lags(), column_shapes, TAPS)), axis=1)
     )
     lag = np.arange(rows)[None, :] - np.arange(rows)[:, None]
@@ -168,8 +168,7 @@
             in_specs=[
                 pl.BlockSpec((batch, rows, width), lambda i, *r: (i, 0, 0)),
                 pl.BlockSpec(bank.shape, lambda i, *r: (0, 0, 0)),
-                pl.BlockSpec(top.shape, lambda i, *r: (0, 0)),
-                pl.BlockSpec(rest.shape, lambda i, *r: (0, 0)),
+                pl.BlockSpec(taps.shape, lambda i, *r: (0, 0, 0)),
             ],
             out_specs=[
                 pl.BlockSpec(shape, lambda i, *r: (0, 0, 0, 0)),
@@ -180,11 +179,11 @@
         out_shape=(jax.ShapeDtypeStruct(shape, F32), jax.ShapeDtypeStruct(note, F32)),
         compiler_params=pltpu.CompilerParams(vmem_limit_bytes=50 * 2**20),
         name="match",
-    )(routes, offsets, weights, coeffs.reshape(-1), pieces, jnp.asarray(bank), top, rest)
+    )(routes, offsets, weights, coeffs.reshape(-1), pieces, jnp.asarray(bank), taps)
 
 
 def combine_body(
-    tiles, quarters, note_ref, sent_ref, top_ref, rest_ref, band_top_ref, band_rest_ref,
+    tiles, quarters, note_ref, sent_ref, taps_ref, band_ref,
     coadd_ref, out_ref,
     landed, notes, select, part, right, left, sheet, inverse,
     note_send, note_recv, ring_send, ring_recv, right_send, right_recv, left_send, left_recv, rim_send, rim_recv,
@@ -416,13 +415,13 @@
         def _():
             rim(c, False).wait_recv()
 
-    b_top, b_rest = band_top_ref[...], band_rest_ref[...]
+    b_top, b_rest = band_ref[0], band_ref[1]
     columns = []
     for c in range(chunks):
         s_top, s_rest = halves(sheet[c])
         columns.append(dot(b_top, s_top) + (dot(b_rest, s_top) + dot(b_top, s_rest)))
     top, rest = halves(windows_of(jnp.concatenate(columns, axis=1)))
-    swept = dot(top, top_ref[...]) + (dot(rest, top_ref[...]) + dot(top, rest_ref[...]))
+    swept = dot(top, taps_ref[0]) + (dot(rest, taps_ref[0]) + dot(top, taps_ref[1]))
     for j in range(out_ref.shape[1] // LANES):
         out_ref[:, j * LANES : (j + 1) * LANES] = swept[j * own : (j + 1) * own]
 
@@ -459,9 +458,9 @@
     chunks, _, span, chunk = sent.shape
     width = chunks * chunk
     own = SR // quarters
-    top, rest = halves_np(detect_taps(window_lags(), REACH))
+    taps = halves_np(detect_taps(window_lags(), REACH))
     lag = np.arange(own + 2 * RIM)[None, :] - RIM - np.arange(own)[:, None]
-    band_top, band_rest = halves_np(detect_taps(lag, REACH))
+    band = halves_np(detect_taps(lag, REACH))
     result = jax.ShapeDtypeStruct((own, width), F32)
     held = pltpu.VMEM((chunks, quarters, own, chunk), F32)
     every = pltpu.SemaphoreType.DMA((tiles * quarters,))
@@ -471,7 +470,7 @@
     return pl.pallas_call(
         functools.partial(combine_body, tiles, quarters),
         out_shape=(result, result),
-        in_specs=[pl.BlockSpec(memory_space=pltpu.VMEM)] * 6,
+        in_specs=[pl.BlockSpec(memory_space=pltpu.VMEM)] * 4,
         out_specs=[pl.BlockSpec(memory_space=pltpu.VMEM)] * 2,
         scratch_shapes=[
             pltpu.VMEM(sent.shape, F32),
@@ -488,7 +487,7 @@
             vmem_limit_bytes=52 * 2**20, collective_id=0, has_side_effects=True
         ),
         name="combine",
-    )(note, sent, top, rest, band_top, band_rest)
+    )(note, sent, taps, band)
 
 
 def shards(pieces, coeffs, weights, routes, offsets):

time: 131 us -> 126 us (0.962)
  Pallas kernels: 116 us -> 113 us
  local copies, waits for them, and re-layouts: 14.1 us -> 11.6 us
    pallas_call x1, Pallas kernels: 107 us -> 104 us  [combine(): pl.pallas_call(functools.partial(combine_body, tiles, quarters), out_shap...]
    unnamed x25 -> x19, local copies, waits for them, and re-layouts: 14 us -> 11.5 us
where the time goes in v4:
time: 126 us; the launch traced here: 125 us
  Pallas kernels  113 us (90%)
  local copies, waits for them, and re-layouts  11.6 us (9%)
    pallas_call x1, Pallas kernels, combine(): pl.pallas_call(functools.partial(combine_body, tiles, quarters), out_shap...  104 us
    unnamed x19, local copies, waits for them, and re-layouts  11.5 us
    pallas_call x1, Pallas kernels, match(): pl.pallas_call(functools.partial(match_body, capacity), grid_spec=pltpu.P...  9.09 us

profile of v4, /device:TPU:4, one launch (start us, length us, event | category | flops | bytes accessed | tf_op | source)
XLA Modules:
  0.0 125.4 jit_solution(17454715525900592429)
XLA Ops:
  0.6 0.8 copy.11
  1.5 0.1 reshape.10.coeffs_ref
  1.6 0.0 copy-start
  1.6 1.6 %copy-done = f32[32,16,1024]{2,1,0:T(8,128)S(1)} copy-done((f32[32,16,1024]{2,1,0:T(8,128)S(1)}, f32[32,16,1024]{2,1,0:T(8,128)}, u32[]{:S(2)}) %copy-start) | copy-done | bytes 2097176
  3.2 0.0 copy-start.1
  3.2 1.0 copy-done.1
  4.2 0.0 copy-start.4
  4.2 0.9 copy-done.4
  5.1 0.0 copy-start.5
  5.1 0.7 copy-done.5
  5.7 0.0 copy-start.6
  5.7 0.7 copy-done.6
  6.4 0.0 copy-start.7
  6.4 0.7 copy-done.7
  7.1 9.1 %match.1 = (f32[8,64,16,128]{3,2,1,0:T(8,128)}, f32[8,8,128]{2,1,0:T(8,128)S(1)}) custom-call(s32[32]{0:T(128)S(1)} %bitcast.2, s32[32]{0:T(128)S(1)} %copy-done.6, f32[32]{0:T(128)S(1)} %copy-done.7, f32[640]{0:T(1024)S(1)} %reshape.10.coeffs_ref, f32[32,16,1024]{2,1,0:T(8,128)S(1)} %copy-done, f32[5,16,256]{2,1,0:T(8,128)S(1)} %copy-done.4, ...), custom_call_target="tpu_custom_call" | custom-call | tf_op jit(solution)/shard_map/match/pallas_call | solution.py:163
  16.2 0.0 copy-start.2
  16.2 1.0 copy-done.2
  17.1 0.0 copy-start.3
  17.2 0.9 copy-done.3
  18.1 104.0 %combine.1 = (f32[256,1024]{1,0:T(8,128)S(1)}, f32[256,1024]{1,0:T(8,128)}) custom-call(f32[8,8,128]{2,1,0:T(8,128)S(1)} %get-tuple-element.4.note_ref, f32[8,8,128,128]{3,2,1,0:T(8,128)} %bitcast.3, bf16[2,256,128]{2,1,0:T(8,128)(2,1)S(1)} %copy-done.3, bf16[2,256,288]{2,1,0:T(8,128)(2,1)S(1)} %copy-done.2), custom_call_target="tpu_custom_call" | custom-call | tf_op jit(solution)/shard_map/combine/pallas_call | solution.py:470
  122.1 1.0 copy.14
  123.1 2.3 %copy.15 = f32[256,1024]{1,0:T(8,128)} copy(f32[256,1024]{1,0:T(8,128)} %get-tuple-element.9) | data formatting | bytes 2097152
Async XLA Ops:
  1.6 1.6 %copy-start = (f32[32,16,1024]{2,1,0:T(8,128)S(1)}, f32[32,16,1024]{2,1,0:T(8,128)}, u32[]{:S(2)}) copy-start(f32[32,16,1024]{2,1,0:T(8,128)} %pieces_ref.1) | copy-start | bytes 6291460
  3.2 1.0 copy-start.1
  4.2 0.9 copy-start.4
  5.1 0.7 copy-start.5
  5.7 0.7 copy-start.6
  6.4 0.7 copy-start.7
  16.2 1.0 copy-start.2
  17.1 0.9 copy-start.3
